TPU v7x, 32 devices: a whole 2x2x4 slice. The times are simulated.
32 devices in a mesh: dp: 8 (over y, x, core), ctx: 4 (over z).
Axes of the slice: x: 2, y: 2, z: 4, core: 2. Of those that a mesh axis runs over, the one named last changes fastest.
Arguments:
- hidden: bfloat16 [8, 512, 3584], P('dp', 'ctx'), may hold values from -6 to 6
- norm_gain: bfloat16 [3584], replicated, may hold values from 0.099609375 to 1.8984375
- w_query: bfloat16 [3584, 2048], P('dp'), may hold values from -0.09375 to 0.09375
- w_key: bfloat16 [3584, 512], P('dp'), may hold values from -0.09375 to 0.09375
- w_value: bfloat16 [3584, 512], P('dp'), may hold values from -0.09375 to 0.09375
- bias_query: bfloat16 [2048], replicated, may hold values from -4 to 4
- bias_key: bfloat16 [512], replicated, may hold values from -4 to 4
- bias_value: bfloat16 [512], replicated, may hold values from -4 to 4
- kv_blocks: int32 [16, 4, 4], P('ctx'), may hold values from 0 to 3, as said below
- block_counts: int32 [16, 4], P('ctx'), may hold values from 1 to 4, as said below
Outputs:
- attended: bfloat16 [8, 512, 2048], P('dp', 'ctx')
Inputs may be any that keep to these rules, and one draw needn't show every extreme that they name: Entry 0 of kv_blocks[h, b] is b itself; entries 1 to block_counts[h, b] - 1 are distinct blocks below b; later entries are valid block numbers that are not used. block_counts[h, b] is at most b + 1, and the last query block of every head has 4.
All inputs are finite; a program needn't handle non-finite values.
Results may differ from a plain program's by a relative error of at most 0.0053.
Values may be sent and summed in bfloat16 or wider, within the bound.
A program may use at most 64 MiB of HBM per device.

v0:
```python
import jax
import jax.numpy as jnp
from jax import lax
from jax.sharding import PartitionSpec as P

KVH = 4
HEAD = 128
QHEADS = 16
BLOCK = 128
MAXB = 4


EPSILON = 1e-06
THETA = 1000000.0


def rms_norm(tokens, norm_gain):
    floats = tokens.astype(jnp.float32)
    meansq = jnp.mean(floats * floats, axis=-1, keepdims=True)
    return (floats * lax.rsqrt(meansq + EPSILON) * norm_gain.astype(jnp.float32)).astype(
        jnp.bfloat16
    )


def rotary(heads_in, position):
    half_size = heads_in.shape[-1] // 2
    exponent = jnp.arange(half_size, dtype=jnp.float32) * (2.0 / heads_in.shape[-1])
    inverse = jnp.power(jnp.float32(THETA), -exponent)
    angles = position[:, None] * inverse[None, :]
    cosine = jnp.cos(angles)[:, None, :]
    sine = jnp.sin(angles)[:, None, :]
    first = heads_in[..., :half_size]
    second = heads_in[..., half_size:]
    return jnp.concatenate(
        [first * cosine - second * sine, second * cosine + first * sine], axis=-1
    )


def finish_heads(summed, bias, heads, position, rotate_it):
    shaped = (summed + bias.astype(jnp.float32)).reshape(summed.shape[0], heads, HEAD)
    if rotate_it:
        shaped = rotary(shaped, position)
    return shaped.astype(jnp.bfloat16)


def fold_rows(source, pieces):
    return tuple((jnp.dot(source, piece, preferred_element_type=jnp.float32) for piece in pieces))


def sparse_head(queries, key_rows, value_rows, blocks, counts):
    nblocks = queries.shape[0] // BLOCK
    query_tiles = queries.reshape(nblocks, BLOCK, HEAD)
    key_tiles = key_rows.reshape(nblocks, BLOCK, HEAD)[blocks].reshape(nblocks, MAXB * BLOCK, HEAD)
    value_tiles = value_rows.reshape(nblocks, BLOCK, HEAD)[blocks].reshape(
        nblocks, MAXB * BLOCK, HEAD
    )
    scores = jnp.einsum(
        "qih,qjh->qij", query_tiles, key_tiles, preferred_element_type=jnp.float32
    ) * HEAD ** (-0.5)
    column = jnp.arange(MAXB * BLOCK)
    slot_of = column // BLOCK
    inside = column % BLOCK
    row_pos = jnp.arange(BLOCK)
    allowed = (slot_of[None, None, :] < counts[:, None, None]) & (
        (slot_of[None, None, :] > 0) | (inside[None, None, :] <= row_pos[None, :, None])
    )
    expo = jnp.where(allowed, jnp.exp(scores), jnp.float32(0.0))
    totals = jnp.sum(expo, axis=-1)
    probs = expo.astype(jnp.bfloat16)
    mixed = (
        jnp.einsum("qij,qjh->qih", probs, value_tiles, preferred_element_type=jnp.float32)
        / totals[..., None]
    )
    return mixed.astype(jnp.bfloat16).reshape(nblocks * BLOCK, HEAD)


def one_head(packed):
    return sparse_head(packed[0], packed[1], packed[2], packed[3], packed[4])


def body(
    hidden,
    norm_gain,
    w_query,
    w_key,
    w_value,
    bias_query,
    bias_key,
    bias_value,
    kv_blocks,
    block_counts,
):
    groups = lax.axis_size("ctx")
    device = lax.axis_index("ctx")
    tokens = hidden[0]
    local_rows = tokens.shape[0]
    seq_len = local_rows * groups
    heads_here = QHEADS // groups
    kv_here = KVH // groups
    width_query = heads_here * HEAD
    width_pair = kv_here * HEAD
    normed = rms_norm(tokens, norm_gain)
    sum_query, sum_key, sum_value = fold_rows(
        normed,
        (
            lax.all_gather(w_query, "dp", axis=0, tiled=True),
            lax.all_gather(w_key, "dp", axis=0, tiled=True),
            lax.all_gather(w_value, "dp", axis=0, tiled=True),
        ),
    )
    position = (device * local_rows + jnp.arange(local_rows, dtype=jnp.int32)).astype(jnp.float32)
    queries = finish_heads(sum_query, bias_query, QHEADS, position, True)
    key_rows = finish_heads(sum_key, bias_key, KVH, position, True)
    value_rows = finish_heads(sum_value, bias_value, KVH, position, False)
    query_send = queries.reshape(local_rows, groups, width_query)
    pair_send = jnp.concatenate([key_rows, value_rows], axis=2)
    query_got, pair_got = (
        lax.all_to_all(query_send, "ctx", split_axis=1, concat_axis=0, tiled=True),
        lax.all_to_all(pair_send, "ctx", split_axis=1, concat_axis=0, tiled=True),
    )
    queries = query_got.reshape(seq_len, heads_here, HEAD)
    key_rows = pair_got[:, 0, :width_pair].reshape(seq_len, kv_here, HEAD)
    value_rows = pair_got[:, 0, width_pair:].reshape(seq_len, kv_here, HEAD)
    group = heads_here // kv_here
    key_rows = jnp.repeat(key_rows, group, axis=1)
    value_rows = jnp.repeat(value_rows, group, axis=1)
    mixed = lax.map(
        one_head,
        (
            queries.transpose(1, 0, 2),
            key_rows.transpose(1, 0, 2),
            value_rows.transpose(1, 0, 2),
            kv_blocks,
            block_counts,
        ),
    )
    result = mixed.transpose(1, 0, 2).reshape(seq_len, 1, width_query)
    returned = lax.all_to_all(result, "ctx", split_axis=0, concat_axis=1, tiled=True)
    return returned.reshape(1, local_rows, QHEADS * HEAD)


def solution(mesh):
    placed = (
        P("dp", "ctx", None),
        P(),
        P("dp", None),
        P("dp", None),
        P("dp", None),
        P(),
        P(),
        P(),
        P("ctx", None, None),
        P("ctx", None),
    )
    return jax.shard_map(
        body, mesh=mesh, in_specs=placed, out_specs=P("dp", "ctx", None), check_vma=False
    )
```

profile of v0, /device:TPU:25, one launch (start us, length us, event | category | flops | bytes accessed | tf_op | source)
XLA Modules:
  0.0 234.1 jit_solution(543482916800295101)
XLA Ops:
  6.6 0.7 all-gather.8.cloned.1.call-update
  7.3 0.7 all-gather.6.cloned.1.call-update
  8.1 0.7 all-gather.4.cloned.1.call-update
  9.6 35.6 %all-gather.8.cloned.1.call-done = bf16[3584,512]{1,0:T(8,128)(2,1)} async-done(((bf16[448,512]{1,0:T(8,128)(2,1)}), bf16[3584,512]{1,0:T(8,128)(2,1)}) %all-gather.8.cloned.1.call-update) | async-done | bytes 3670032 | tf_op jit(solution)/shard_map/all_gather | solution.py:108
  45.2 2.7 %fusion.17 = bf16[16,4,8,128]{3,2,1,0:T(8,128)(2,1)S(1)} fusion(bf16[3584,512]{1,0:T(8,128)(2,1)} %all-gather.8.cloned.1.call-done, f32[512]{0:T(512)S(1)} %convert_element_type.60, bf16[1,128,3584]{2,1,0:T(8,128)(2,1)S(1)} %copy-done, f32[3584]{0:T(1024)S(1)} %convert_element_type.54, f32[128]{0:T(128)S(1)} %add_rsqrt_fusion), kind=kOutput, calls=%fused_computation.40 | convolution fusion | flops 471728128 | bytes 4735488 | tf_op jit(solution)/shard_map/dot_general | solution.py:47
  48.0 33.7 %all-gather.6.cloned.1.call-done = bf16[3584,512]{1,0:T(8,128)(2,1)} async-done(((bf16[448,512]{1,0:T(8,128)(2,1)}), bf16[3584,512]{1,0:T(8,128)(2,1)}) %all-gather.6.cloned.1.call-update) | async-done | bytes 3670032 | tf_op jit(solution)/shard_map/all_gather | solution.py:107
  81.7 2.7 %convolution_add_fusion.2 = f32[128,512]{1,0:T(8,128)S(1)} fusion(bf16[3584,512]{1,0:T(8,128)(2,1)} %all-gather.6.cloned.1.call-done, f32[512]{0:T(512)S(1)} %convert_element_type.59, bf16[1,128,3584]{2,1,0:T(8,128)(2,1)S(1)} %copy-done, f32[3584]{0:T(1024)S(1)} %convert_element_type.54, f32[128]{0:T(128)S(1)} %add_rsqrt_fusion), kind=kOutput, calls=%fused_computation.38 | convolution fusion | flops 471662592 | bytes 4866560 | tf_op jit(solution)/shard_map/dot_general | solution.py:47
  84.8 0.9 pad_maximum_fusion.1
  85.6 4.5 %all-to-all-start.1 = ((bf16[128,4,256]{2,0,1:T(8,128)(2,1)}), bf16[128,4,256]{2,0,1:T(8,128)(2,1)S(1)}, u32[]{:S(2)}, u32[]{:S(2)}) async-start(bf16[128,4,256]{2,0,1:T(8,128)(2,1)} %pad_maximum_fusion.1), calls=%async_computation.1 | async-start | bytes 524288 | tf_op jit(solution)/shard_map/all_to_all | solution.py:119
  90.2 74.4 %all-gather.4.cloned.1.call-done = bf16[3584,2048]{1,0:T(8,128)(2,1)} async-done(((bf16[448,2048]{1,0:T(8,128)(2,1)}), bf16[3584,2048]{1,0:T(8,128)(2,1)}) %all-gather.4.cloned.1.call-update) | async-done | bytes 14680080 | tf_op jit(solution)/shard_map/all_gather | solution.py:106
  164.6 7.3 %convolution_add_fusion = f32[128,2048]{1,0:T(8,128)S(1)} fusion(bf16[3584,2048]{1,0:T(8,128)(2,1)} %all-gather.4.cloned.1.call-done, f32[2048]{0:T(1024)S(1)} %convert_element_type.56, bf16[1,128,3584]{2,1,0:T(8,128)(2,1)S(1)} %copy-done, f32[3584]{0:T(1024)S(1)} %convert_element_type.54, f32[128]{0:T(128)S(1)} %add_rsqrt_fusion), kind=kOutput, calls=%fused_computation.31 | convolution fusion | flops 1881145344 | bytes 16669184 | tf_op jit(solution)/shard_map/dot_general | solution.py:47
  171.9 0.3 copy.43
  172.4 0.8 pad_maximum_fusion
  173.2 4.5 %all-to-all-start = ((bf16[128,4,512]{0,2,1:T(8,128)(2,1)}), bf16[128,4,512]{0,2,1:T(8,128)(2,1)S(1)}, u32[]{:S(2)}, u32[]{:S(2)}) async-start(bf16[128,4,512]{0,2,1:T(8,128)(2,1)} %bitcast.10), calls=%async_computation | async-start | bytes 1048576 | tf_op jit(solution)/shard_map/all_to_all | solution.py:118
  177.8 12.0 %all-to-all-done = bf16[128,4,512]{0,2,1:T(8,128)(2,1)S(1)} async-done(((bf16[128,4,512]{0,2,1:T(8,128)(2,1)}), bf16[128,4,512]{0,2,1:T(8,128)(2,1)S(1)}, u32[]{:S(2)}, u32[]{:S(2)}) %all-to-all-start) | async-done | bytes 524320 | tf_op jit(solution)/shard_map/all_to_all | solution.py:118
  190.3 0.7 copy-done.1
  191.0 15.8 %while.12 = (s32[]{:T(128)}, bf16[4,512,128]{1,2,0:T(8,128)(2,1)S(1)}, s32[4,4]{1,0:T(4,128)}, bf16[4,512,128]{2,1,0:T(8,128)(2,1)S(1)}, bf16[4,512,128]{2,1,0:T...) while((s32[]{:T(128)}, bf16[4,512,128]{1,2,0:T(8,128)(2,1)S(1)}, ...), condition=%wide.region_3.4_spmd, body=%wide.region_1.3_spmd.sunk | while | flops 135803952 | bytes 5920353 | solution.py:127
  191.0 0.7 compare_select_fusion.2
  191.8 0.6 gather_fusion
  192.5 0.6 gather_fusion.1
  193.2 0.7 fusion.45
  194.0 0.5 fusion.46
  194.5 0.3 fusion.47
  195.0 0.7 compare_select_fusion.2
  195.8 0.6 gather_fusion
  196.4 0.6 gather_fusion.1
  197.2 0.7 fusion.45
  197.9 0.5 fusion.46
  198.4 0.3 fusion.47
  198.9 0.7 compare_select_fusion.2
  199.7 0.6 gather_fusion
  200.4 0.6 gather_fusion.1
  201.1 0.7 fusion.45
  201.9 0.5 fusion.46
  202.4 0.3 fusion.47
  202.9 0.7 compare_select_fusion.2
  203.7 0.6 gather_fusion
  204.4 0.6 gather_fusion.1
  205.1 0.7 fusion.45
  205.9 0.5 fusion.46
  206.4 0.3 fusion.47
  206.8 0.5 broadcast.299
  207.3 1.0 reduce
  208.6 0.4 reshape.302
  209.0 16.7 %all_to_all.48 = bf16[4,2,32768]{2,1,0:T(2,128)(2,1)S(1)} all-to-all(bf16[4,2,32768]{2,1,0:T(2,128)(2,1)S(1)} %reshape.302), channel_id=1, replica_groups=mesh['dp'=8,'ctx'=4] {'ctx'}, dimensions={0} | all-to-all | bytes 1048576 | tf_op jit(solution)/shard_map/all_to_all | solution.py:138
  225.7 0.5 reshape.303
  226.3 0.3 copy.41
  226.6 1.0 copy.42
  (80 shorter events, 3.9 us)
Async XLA Ops:
  6.5 2.2 copy-start.3
  6.5 2.3 copy-start.2
  6.5 2.3 copy-start.4
  6.5 2.3 copy-start.5
  6.5 2.7 %copy-start = (bf16[1,128,3584]{2,1,0:T(8,128)(2,1)S(1)}, bf16[1,128,3584]{2,1,0:T(8,128)(2,1)}, u32[]{:S(2)}) copy-start(bf16[1,128,3584]{2,1,0:T(8,128)(2,1)} %param.12) | copy-start | bytes 2752516
  6.5 38.7 %all-gather.8.cloned.1.call-start = ((), (), s32[]{:S(2)}) async-start(), calls=%async_computation.5 | async-start | bytes 4128768 | tf_op jit(solution)/shard_map/all_gather | solution.py:108
  7.3 74.4 %all-gather.6.cloned.1.call-start = ((), (), s32[]{:S(2)}) async-start(), calls=%async_computation.4 | async-start | bytes 4128768 | tf_op jit(solution)/shard_map/all_gather | solution.py:107
  8.0 156.5 %all-gather.4.cloned.1.call-start = ((), (), s32[]{:S(2)}) async-start(), calls=%async_computation.3 | async-start | bytes 16515072 | tf_op jit(solution)/shard_map/all_gather | solution.py:106
  85.6 87.6 %all-to-all-start.1 = ((bf16[128,4,256]{2,0,1:T(8,128)(2,1)}), bf16[128,4,256]{2,0,1:T(8,128)(2,1)S(1)}, u32[]{:S(2)}, u32[]{:S(2)}) async-start(bf16[128,4,256]{2,0,1:T(8,128)(2,1)} %pad_maximum_fusion.1), calls=%async_computation.1 | async-start | bytes 524288 | tf_op jit(solution)/shard_map/all_to_all | solution.py:119
  173.2 16.5 %all-to-all-start = ((bf16[128,4,512]{0,2,1:T(8,128)(2,1)}), bf16[128,4,512]{0,2,1:T(8,128)(2,1)S(1)}, u32[]{:S(2)}, u32[]{:S(2)}) async-start(bf16[128,4,512]{0,2,1:T(8,128)(2,1)} %bitcast.10), calls=%async_computation | async-start | bytes 1048576 | tf_op jit(solution)/shard_map/all_to_all | solution.py:118
  189.9 1.0 copy-start.1
Sparse Core Ops, SparseCore 0:
  9.3 35.9 all-gather.7
  47.1 34.5 all-gather.5
  83.6 80.9 all-gather.3
where the time goes:
time: 239 us; the launch traced here: 234 us
  waiting for transfers between devices  158 us (66%)
  blocking collectives  16.7 us (7%)
  matrix products  15.9 us (7%)
  local copies, waits for them, and re-layouts  14.1 us (6%)
  between operations  13.4 us (6%)
  starting transfers between devices  9.18 us (4%)
  other arithmetic  6.78 us (3%)
    all_gather x1, waiting for transfers between devices, body(): lax.all_gather(w_query, 'dp', axis=0, tiled=True)  74.4 us
    all_gather x1, waiting for transfers between devices, body(): lax.all_gather(w_value, 'dp', axis=0, tiled=True)  35.6 us
    all_gather x1, waiting for transfers between devices, body(): lax.all_gather(w_key, 'dp', axis=0, tiled=True)  33.7 us
    all_to_all x1, blocking collectives, body(): lax.all_to_all(result, 'ctx', split_axis=0, concat_axis=1, tiled=True)  16.7 us
    dot_general x3, matrix products, fold_rows(): jnp.dot(source, piece, preferred_element_type=jnp.float32)  12.8 us
    all_to_all x1, waiting for transfers between devices, body(): lax.all_to_all(query_send, 'ctx', split_axis=1, concat_axis=0, tiled=True)  12 us
  transfers between devices with their start and end apart: 5, of which 4 were waited for; matrix products, arithmetic and copies ran while one was open for 7% of the time, Pallas kernels for 0%

commit v1 on v0

--- a/solution.py
+++ b/solution.py
@@ -100,13 +100,19 @@
     width_query = heads_here * HEAD
     width_pair = kv_here * HEAD
     normed = rms_norm(tokens, norm_gain)
-    sum_query, sum_key, sum_value = fold_rows(
-        normed,
-        (
-            lax.all_gather(w_query, "dp", axis=0, tiled=True),
-            lax.all_gather(w_key, "dp", axis=0, tiled=True),
-            lax.all_gather(w_value, "dp", axis=0, tiled=True),
-        ),
+    parts = lax.axis_size("dp")
+    depth = w_query.shape[0]
+    gathered = lax.all_to_all(
+        normed.reshape(local_rows, parts, depth), "dp", split_axis=1, concat_axis=0, tiled=True
+    ).reshape(parts * local_rows, depth)
+    weights = jnp.concatenate([w_key, w_value, w_query], axis=1)
+    partial = jnp.dot(gathered, weights, preferred_element_type=jnp.float32).astype(jnp.bfloat16)
+    summed = lax.psum_scatter(partial, "dp", scatter_dimension=0, tiled=True).astype(jnp.float32)
+    width = KVH * HEAD
+    sum_key, sum_value, sum_query = (
+        summed[:, :width],
+        summed[:, width : 2 * width],
+        summed[:, 2 * width :],
     )
     position = (device * local_rows + jnp.arange(local_rows, dtype=jnp.int32)).astype(jnp.float32)
     queries = finish_heads(sum_query, bias_query, QHEADS, position, True)

time: 239 us -> 172 us (0.72)
  the two profiles are of different devices: /device:TPU:25 before, /device:TPU:0 now
where the time goes in v1:
time: 172 us
  waiting for transfers between devices  80.7 us (47%)
  blocking collectives  34.8 us (20%)
  local copies, waits for them, and re-layouts  16.3 us (9%)
  between operations  13.7 us (8%)
  matrix products  9.01 us (5%)
  other arithmetic  8.97 us (5%)
  starting transfers between devices  8.08 us (5%)
    reduce_scatter x1, waiting for transfers between devices, body(): lax.psum_scatter(partial, 'dp', scatter_dimension=0, tiled=True)  60.1 us
    all_to_all x1, blocking collectives, body(): lax.all_to_all(normed.reshape(local_rows, parts, depth), 'dp', split_axis...  19.1 us
    all_to_all x1, blocking collectives, body(): lax.all_to_all(result, 'ctx', split_axis=0, concat_axis=1, tiled=True)  15.7 us
    all_to_all x1, waiting for transfers between devices, body(): lax.all_to_all(query_send, 'ctx', split_axis=1, concat_axis=0, tiled=True)  13.1 us
    all_to_all x1, waiting for transfers between devices, body(): lax.all_to_all(pair_send, 'ctx', split_axis=1, concat_axis=0, tiled=True)  7.49 us
    dot_general x1, matrix products, body(): jnp.dot(gathered, weights, preferred_element_type=jnp.float32)  5.81 us
    all_to_all x1, starting transfers between devices, body(): lax.all_to_all(pair_send, 'ctx', split_axis=1, concat_axis=0, tiled=True)  4.61 us
    unnamed x19, local copies, waits for them, and re-layouts  3.47 us
  transfers between devices with their start and end apart: 3, of which 3 were waited for; matrix products, arithmetic and copies ran while one was open for 1% of the time, Pallas kernels for 0%

profile of v1, /device:TPU:0, one launch (start us, length us, event | category | flops | bytes accessed | tf_op | source)
XLA Modules:
  0.0 171.8 jit_solution(2758312384831453663)
XLA Ops:
  6.5 1.6 copy.34
  8.1 0.5 multiply_reduce_fusion
  8.7 0.5 multiply_convert_fusion
  9.2 19.1 %all_to_all.63 = bf16[128,8,448]{0,2,1:T(8,128)(2,1)S(1)} all-to-all(bf16[128,8,448]{0,2,1:T(8,128)(2,1)S(1)} %multiply_convert_fusion), channel_id=1, replica_groups=mesh['dp'=8,'ctx'=4] {'dp'}, dimensions={1} | all-to-all | bytes 1835008 | tf_op jit(solution)/shard_map/all_to_all | solution.py:105
  28.3 0.6 copy.35
  28.9 5.8 %convolution_convert_fusion = bf16[1024,3072]{1,0:T(8,128)(2,1)} fusion(bf16[448,2048]{1,0:T(8,128)(2,1)S(1)} %copy-done.4, bf16[448,512]{1,0:T(8,128)(2,1)S(1)} %copy-done.5, bf16[448,512]{1,0:T(8,128)(2,1)S(1)} %copy-done.6, bf16[56,8,8,128]{3,2,1,0:T(8,128)(2,1)S(1)} %bitcast.97), kind=kOutput, calls=%fused_computation.31 | convolution fusion | flops 2829975552 | bytes 9961472 | tf_op jit(solution)/shard_map/dot_general | solution.py:109
  34.8 0.6 copy-done.2
  35.9 60.1 %reduce-scatter.2.cloned.1.call-done = bf16[128,3072]{1,0:T(8,128)(2,1)} async-done(((bf16[1024,3072]{1,0:T(8,128)(2,1)}), bf16[128,3072]{1,0:T(8,128)(2,1)}) %reduce-scatter.2.cloned.1.call-update) | async-done | bytes 786448 | tf_op jit(solution)/shard_map/reduce_scatter | solution.py:110
  96.0 1.3 convert_element_type.66
  97.8 0.9 pad_maximum_fusion.1
  98.6 4.6 %all-to-all-start.2 = ((bf16[128,4,256]{2,0,1:T(8,128)(2,1)}), bf16[128,4,256]{2,0,1:T(8,128)(2,1)S(1)}, u32[]{:S(2)}, u32[]{:S(2)}) async-start(bf16[128,4,256]{2,0,1:T(8,128)(2,1)} %pad_maximum_fusion.1), calls=%async_computation.3 | async-start | bytes 524288 | tf_op jit(solution)/shard_map/all_to_all | solution.py:125
  103.4 0.3 copy.49
  103.9 0.8 pad_maximum_fusion
  104.7 7.5 %all-to-all-done.2 = bf16[128,4,256]{2,0,1:T(8,128)(2,1)S(1)} async-done(((bf16[128,4,256]{2,0,1:T(8,128)(2,1)}), bf16[128,4,256]{2,0,1:T(8,128)(2,1)S(1)}, u32[]{:S(2)}, u32[]{:S(2)}) %all-to-all-start.2) | async-done | bytes 262176 | tf_op jit(solution)/shard_map/all_to_all | solution.py:125
  112.2 3.5 %all-to-all-start.1 = ((bf16[128,4,512]{0,2,1:T(8,128)(2,1)}), bf16[128,4,512]{0,2,1:T(8,128)(2,1)S(1)}, u32[]{:S(2)}, u32[]{:S(2)}) async-start(bf16[128,4,512]{0,2,1:T(8,128)(2,1)} %bitcast.11), calls=%async_computation.2 | async-start | bytes 1048576 | tf_op jit(solution)/shard_map/all_to_all | solution.py:124
  115.7 13.1 %all-to-all-done.1 = bf16[128,4,512]{0,2,1:T(8,128)(2,1)S(1)} async-done(((bf16[128,4,512]{0,2,1:T(8,128)(2,1)}), bf16[128,4,512]{0,2,1:T(8,128)(2,1)S(1)}, u32[]{:S(2)}, u32[]{:S(2)}) %all-to-all-start.1) | async-done | bytes 524320 | tf_op jit(solution)/shard_map/all_to_all | solution.py:124
  129.3 15.8 %while.12 = (s32[]{:T(128)}, bf16[4,512,128]{1,2,0:T(8,128)(2,1)S(1)}, s32[4,4]{1,0:T(4,128)}, bf16[4,512,128]{2,1,0:T(8,128)(2,1)S(1)}, bf16[4,512,128]{2,1,0:T...) while((s32[]{:T(128)}, bf16[4,512,128]{1,2,0:T(8,128)(2,1)S(1)}, ...), condition=%wide.region_4.5_spmd, body=%wide.region_2.4_spmd.sunk | while | flops 135803952 | bytes 5920345 | solution.py:133
  129.4 0.7 compare_select_fusion.2
  130.2 0.6 gather_fusion.1
  130.8 0.7 fusion.44
  131.7 0.5 fusion.45
  132.2 0.7 gather_fusion
  132.8 0.3 fusion.46
  133.3 0.7 compare_select_fusion.2
  134.1 0.6 gather_fusion.1
  134.8 0.7 fusion.44
  135.6 0.5 fusion.45
  136.1 0.7 gather_fusion
  136.8 0.3 fusion.46
  137.3 0.7 compare_select_fusion.2
  138.1 0.6 gather_fusion.1
  138.7 0.7 fusion.44
  139.6 0.5 fusion.45
  140.1 0.7 gather_fusion
  140.8 0.3 fusion.46
  141.3 0.7 compare_select_fusion.2
  142.0 0.6 gather_fusion.1
  142.7 0.7 fusion.44
  143.6 0.5 fusion.45
  144.1 0.7 gather_fusion
  144.7 0.3 fusion.46
  145.2 0.5 broadcast.304
  145.7 1.0 reduce.1
  146.9 0.4 reshape.323
  147.3 15.7 %all_to_all.64 = bf16[4,2,32768]{2,1,0:T(2,128)(2,1)S(1)} all-to-all(bf16[4,2,32768]{2,1,0:T(2,128)(2,1)S(1)} %reshape.323), channel_id=1, replica_groups=mesh['dp'=8,'ctx'=4] {'ctx'}, dimensions={0} | all-to-all | bytes 1048576 | tf_op jit(solution)/shard_map/all_to_all | solution.py:144
  163.1 0.5 reshape.324
  163.7 0.3 copy.47
  164.0 1.0 copy.48
  (81 shorter events, 3.7 us)
Async XLA Ops:
  6.5 2.1 %copy-start = (bf16[3584]{0:T(1024)(128)(2,1)S(1)}, bf16[3584]{0:T(1024)(128)(2,1)}, u32[]{:S(2)}) copy-start(bf16[3584]{0:T(1024)(128)(2,1)} %param.13) | copy-start | bytes 21508
  6.5 89.5 %reduce-scatter.2.cloned.1.call-start = ((), (), s32[]{:S(2)}) async-start(), calls=%async_computation.5 | async-start | bytes 7077888 | tf_op jit(solution)/shard_map/reduce_scatter | solution.py:110
  8.7 20.2 %copy-start.4 = (bf16[448,2048]{1,0:T(8,128)(2,1)S(1)}, bf16[448,2048]{1,0:T(8,128)(2,1)}, u32[]{:S(2)}) copy-start(bf16[448,2048]{1,0:T(8,128)(2,1)} %param.14) | copy-start | bytes 5505028
  8.7 20.2 %copy-start.5 = (bf16[448,512]{1,0:T(8,128)(2,1)S(1)}, bf16[448,512]{1,0:T(8,128)(2,1)}, u32[]{:S(2)}) copy-start(bf16[448,512]{1,0:T(8,128)(2,1)} %param.16) | copy-start | bytes 1376260
  8.7 20.2 %copy-start.6 = (bf16[448,512]{1,0:T(8,128)(2,1)S(1)}, bf16[448,512]{1,0:T(8,128)(2,1)}, u32[]{:S(2)}) copy-start(bf16[448,512]{1,0:T(8,128)(2,1)} %param.15) | copy-start | bytes 1376260
  34.7 0.7 copy-start.2
  34.7 0.7 copy-start.3
  34.7 1.1 copy-start.1
  98.6 13.5 %all-to-all-start.2 = ((bf16[128,4,256]{2,0,1:T(8,128)(2,1)}), bf16[128,4,256]{2,0,1:T(8,128)(2,1)S(1)}, u32[]{:S(2)}, u32[]{:S(2)}) async-start(bf16[128,4,256]{2,0,1:T(8,128)(2,1)} %pad_maximum_fusion.1), calls=%async_computation.3 | async-start | bytes 524288 | tf_op jit(solution)/shard_map/all_to_all | solution.py:125
  112.2 16.6 %all-to-all-start.1 = ((bf16[128,4,512]{0,2,1:T(8,128)(2,1)}), bf16[128,4,512]{0,2,1:T(8,128)(2,1)S(1)}, u32[]{:S(2)}, u32[]{:S(2)}) async-start(bf16[128,4,512]{0,2,1:T(8,128)(2,1)} %bitcast.11), calls=%async_computation.2 | async-start | bytes 1048576 | tf_op jit(solution)/shard_map/all_to_all | solution.py:124
Sparse Core Ops, SparseCore 0:
  34.9 61.0 reduce-scatter.1

commit v2 on v1

--- a/solution.py
+++ b/solution.py
@@ -1,6 +1,8 @@
 import jax
 import jax.numpy as jnp
 from jax import lax
+from jax.experimental import pallas as pl
+from jax.experimental.pallas import tpu as pltpu
 from jax.sharding import PartitionSpec as P
 
 KVH = 4
@@ -145,6 +147,438 @@
     return returned.reshape(1, local_rows, QHEADS * HEAD)
 
 
+MESH = pl.DeviceIdType.MESH
+CHUNK = 2 * HEAD
+GROUP = QHEADS // KVH
+PAIRS = KVH // 2
+
+
+def chunk_sources(half, chunk):
+    if chunk < PAIRS:
+        first = pl.multiple_of((PAIRS * half + chunk) * HEAD, HEAD)
+        return ((1, first, HEAD, 0), (2, first, HEAD, HEAD))
+    first = half * (QHEADS // 2 * HEAD) + (chunk - PAIRS) * CHUNK
+    return ((0, pl.multiple_of(first, CHUNK), CHUNK, 0),)
+
+
+def fused_kernel(
+    hidden,
+    gain,
+    w_query,
+    w_key,
+    w_value,
+    bias,
+    cosine,
+    sine,
+    allowed,
+    out,
+    normed,
+    x_buf,
+    w_buf,
+    a1_out,
+    a1_in,
+    b1_out,
+    b1_in,
+    a2_out,
+    a2_in,
+    b2_out,
+    b2_in,
+    keep,
+    own,
+    kv_buf,
+    q_buf,
+    mask_buf,
+    acc,
+    tot,
+    o_buf,
+    o_in,
+    w_loc,
+    w_snd,
+    w_rcv,
+    x_snd,
+    x_rcv,
+    f_snd,
+    f_rcv,
+    m_snd,
+    m_rcv,
+    s1_snd,
+    s1_rcv,
+    s2_snd,
+    s2_rcv,
+    kv_snd,
+    kv_rcv,
+    o_snd,
+    o_rcv,
+):
+    me = lax.axis_index("dp")
+    z = lax.axis_index("ctx")
+    tops = lax.axis_size("ctx")
+    core = lax.rem(me, 2)
+    xpos = lax.rem(me // 2, 2)
+    ypos = me // 4
+    sibling = me + 1 - 2 * core
+    xn = me + 2 - 4 * xpos
+    yn = me + 4 - 8 * ypos
+    dn = xn + 4 - 8 * ypos
+    chunks = w_buf.shape[0]
+    depth = w_query.shape[0]
+    width = 2 * depth
+    weights = (w_query, w_key, w_value)
+    sends = []
+
+    def remote(src, dst, snd, rcv, dp, ctx):
+        return pltpu.make_async_remote_copy(
+            src_ref=src, dst_ref=dst, send_sem=snd, recv_sem=rcv, device_id=(dp, ctx), device_id_type=MESH
+        )
+
+    def launch(*args):
+        copy = remote(*args)
+        copy.start()
+        sends.append(copy)
+
+    locals_ = []
+    rows = pl.ds(pl.multiple_of(core * depth, 64), depth)
+    number = 0
+    for chunk in range(chunks):
+        for which, first, cols, place in chunk_sources(core, chunk):
+            copy = pltpu.make_async_copy(
+                weights[which].at[:, pl.ds(first, cols)],
+                w_buf.at[chunk, rows, pl.ds(place, cols)],
+                w_loc.at[number],
+            )
+            copy.start()
+            locals_.append((chunk, copy))
+            number += 1
+
+    barrier = pltpu.get_barrier_semaphore()
+    for peer in (sibling, xn, yn, dn):
+        pl.semaphore_signal(barrier, inc=1, device_id=(peer, z), device_id_type=MESH)
+    for step in range(1, tops):
+        pl.semaphore_signal(barrier, inc=1, device_id=(me, lax.rem(z + step, tops)), device_id_type=MESH)
+
+    floats = hidden[0].astype(jnp.float32)
+    scale = lax.rsqrt(jnp.mean(floats * floats, axis=-1, keepdims=True) + EPSILON)
+    pl.semaphore_wait(barrier, 4 + tops - 1)
+
+    def norm_block(chip):
+        cols = pl.ds(pl.multiple_of(chip * width, HEAD), width)
+        block = hidden[0, :, cols].astype(jnp.float32)
+        return (block * scale * gain[:, cols].astype(jnp.float32)).astype(jnp.bfloat16)
+
+    relations = (dn, xn, yn)
+    for index, peer in enumerate(relations):
+        normed[index] = norm_block(peer // 2)
+        launch(normed.at[index], x_buf.at[me], x_snd.at[index], x_rcv.at[index], peer, z)
+    x_buf[me] = norm_block(me // 2)
+    launch(x_buf.at[me], x_buf.at[me], f_snd.at[3], f_rcv.at[3], sibling, z)
+
+    number = 0
+    for chunk in range(chunks):
+        for which, first, cols, place in chunk_sources(1 - core, chunk):
+            launch(
+                weights[which].at[:, pl.ds(first, cols)],
+                w_buf.at[chunk, rows, pl.ds(place, cols)],
+                w_snd.at[number],
+                w_rcv.at[number],
+                sibling,
+                z,
+            )
+            number += 1
+    for step in range(1, tops):
+        peer = lax.rem(z + step, tops)
+        launch(allowed.at[peer], mask_buf.at[z], m_snd.at[step - 1], m_rcv.at[step - 1], me, peer)
+    mask_buf[z] = allowed[z]
+
+    def sibling_of(device):
+        return device + 1 - 2 * core
+
+    def docs_of(index):
+        peer = relations[index]
+        remote(x_buf.at[peer], x_buf.at[peer], x_snd.at[index], x_rcv.at[index], peer, z).wait_recv()
+        launch(x_buf.at[peer], x_buf.at[peer], f_snd.at[index], f_rcv.at[index], sibling, z)
+
+    def forwarded(index, device):
+        there = x_buf.at[sibling_of(device)]
+        remote(there, there, f_snd.at[index], f_rcv.at[index], sibling, z).wait_recv()
+
+    def wait_weights(chunk):
+        other = pl.ds(pl.multiple_of((1 - core) * depth, 64), depth)
+        for number, (owner, copy) in enumerate(locals_):
+            if owner == chunk:
+                copy.wait()
+        number = 0
+        for at in range(chunks):
+            for _, _, cols, place in chunk_sources(core, at):
+                if at == chunk:
+                    there = w_buf.at[chunk, other, pl.ds(place, cols)]
+                    remote(there, there, w_snd.at[number], w_rcv.at[number], sibling, z).wait_recv()
+                number += 1
+
+    def product(chunk, device):
+        pair = x_buf[pl.ds(device // 2 * 2, 2)].reshape(2 * BLOCK, width)
+        return jnp.dot(pair, w_buf[chunk], preferred_element_type=jnp.float32)
+
+    def multiply(chunk):
+        wait_weights(chunk)
+        if chunk == 0:
+            forwarded(3, me)
+            docs_of(1)
+            docs_of(2)
+            docs_of(0)
+            forwarded(1, xn)
+        to_x = product(chunk, xn)
+        a1_out[chunk, 0] = to_x[:BLOCK].astype(jnp.bfloat16)
+        keep[chunk, 1] = to_x[BLOCK:]
+        if chunk == 0:
+            forwarded(2, yn)
+        to_y = product(chunk, yn)
+        b1_out[chunk, 0] = to_y[BLOCK:].astype(jnp.bfloat16)
+        keep[chunk, 0] = to_y[:BLOCK]
+        if chunk == 0:
+            forwarded(0, dn)
+        to_d = product(chunk, dn).astype(jnp.bfloat16)
+        a1_out[chunk, 1] = to_d[:BLOCK]
+        b1_out[chunk, 1] = to_d[BLOCK:]
+        launch(a1_out.at[chunk], a1_in.at[chunk], s1_snd.at[0, chunk], s1_rcv.at[0, chunk], xn, z)
+        launch(b1_out.at[chunk], b1_in.at[chunk], s1_snd.at[1, chunk], s1_rcv.at[1, chunk], yn, z)
+        mine = product(chunk, me)
+        own[chunk, 0] = mine[:BLOCK]
+        own[chunk, 1] = mine[BLOCK:]
+
+    def second(chunk):
+        remote(a1_out.at[chunk], a1_in.at[chunk], s1_snd.at[0, chunk], s1_rcv.at[0, chunk], xn, z).wait_recv()
+        a2_out[chunk] = (keep[chunk, 0] + a1_in[chunk, 1].astype(jnp.float32)).astype(jnp.bfloat16)
+        launch(a2_out.at[chunk], a2_in.at[chunk], s2_snd.at[0, chunk], s2_rcv.at[0, chunk], yn, z)
+        remote(b1_out.at[chunk], b1_in.at[chunk], s1_snd.at[1, chunk], s1_rcv.at[1, chunk], yn, z).wait_recv()
+        b2_out[chunk] = (keep[chunk, 1] + b1_in[chunk, 1].astype(jnp.float32)).astype(jnp.bfloat16)
+        launch(b2_out.at[chunk], b2_in.at[chunk], s2_snd.at[1, chunk], s2_rcv.at[1, chunk], xn, z)
+
+    def rotate(head):
+        return (head * cosine[...] + pltpu.roll(head, HEAD // 2, 1) * sine[...]).astype(jnp.bfloat16)
+
+    def kv_copy(pair, origin):
+        place = kv_buf.at[origin, pair]
+        return remote(place, place, kv_snd.at[pair, origin], kv_rcv.at[pair, origin], me, lax.rem(z + 1, tops))
+
+    def finish(chunk):
+        both = ((a1_in, a2_in, a2_out, yn), (b1_in, b2_in, b2_out, xn))
+        for doc, (first_in, second_in, second_out, peer) in enumerate(both):
+            remote(
+                second_out.at[chunk], second_in.at[chunk], s2_snd.at[doc, chunk], s2_rcv.at[doc, chunk], peer, z
+            ).wait_recv()
+            total = (
+                own[chunk, doc]
+                + first_in[chunk, 0].astype(jnp.float32)
+                + second_in[chunk].astype(jnp.float32)
+                + bias[core * chunks + chunk]
+            )
+            if chunk < PAIRS:
+                kv_buf[z, chunk, doc, :, :HEAD] = rotate(total[:, :HEAD])
+                kv_buf[z, chunk, doc, :, HEAD:] = total[:, HEAD:].astype(jnp.bfloat16)
+            else:
+                head = (chunk - PAIRS) * 2
+                q_buf[doc, head] = rotate(total[:, :HEAD])
+                q_buf[doc, head + 1] = rotate(total[:, HEAD:])
+        if chunk < PAIRS:
+
+            @pl.when(z < tops - 1)
+            def _():
+                kv_copy(chunk, z).start()
+
+    def pass_on(pair, step):
+        @pl.when(z >= step)
+        def _():
+            kv_copy(pair, z - step).wait_recv()
+
+            @pl.when(z < tops - 1)
+            def _():
+                kv_copy(pair, z - step).start()
+
+    def scores_of(queries, keys):
+        return lax.dot_general(
+            queries, keys, (((1,), (1,)), ((), ())), preferred_element_type=jnp.float32
+        ) * HEAD ** (-0.5)
+
+    def attend(pair):
+        row = lax.broadcasted_iota(jnp.int32, (BLOCK, BLOCK), 0)
+        column = lax.broadcasted_iota(jnp.int32, (BLOCK, BLOCK), 1)
+        causal = jnp.concatenate([column <= row] * GROUP, axis=0)
+        for doc in range(2):
+            queries = q_buf[doc, pair * GROUP : (pair + 1) * GROUP].reshape(GROUP * BLOCK, HEAD)
+            block = kv_buf[z, pair, doc]
+            expo = jnp.where(causal, jnp.exp(scores_of(queries, block[:, :HEAD])), 0.0)
+            tot[...] = expo
+            acc[...] = jnp.dot(
+                expo.astype(jnp.bfloat16), block[:, HEAD:], preferred_element_type=jnp.float32
+            )
+            for origin in range(tops - 1):
+
+                @pl.when(origin < z)
+                def _():
+                    block = kv_buf[origin, pair, doc]
+                    flags = mask_buf[PAIRS * core + pair]
+                    seen = jnp.concatenate(
+                        [
+                            jnp.broadcast_to(flags[h * tops + origin : h * tops + origin + 1], (BLOCK, BLOCK))
+                            for h in range(GROUP)
+                        ],
+                        axis=0,
+                    )
+                    expo = jnp.where(seen > 0.5, jnp.exp(scores_of(queries, block[:, :HEAD])), 0.0)
+                    tot[...] += expo
+                    acc[...] += jnp.dot(
+                        expo.astype(jnp.bfloat16), block[:, HEAD:], preferred_element_type=jnp.float32
+                    )
+
+            mixed = (acc[...] / jnp.sum(tot[...], axis=-1, keepdims=True)).astype(jnp.bfloat16)
+            for h in range(GROUP):
+                first = h * HEAD
+                o_buf[doc, pair, :, first : first + HEAD] = mixed[h * BLOCK : (h + 1) * BLOCK]
+        launch(o_buf.at[1 - core, pair], o_in.at[pair], o_snd.at[pair], o_rcv.at[pair], sibling, z)
+
+    multiply(0)
+    multiply(1)
+    for chunk in range(chunks):
+        second(chunk)
+        if chunk + 2 < chunks:
+            multiply(chunk + 2)
+        if chunk >= 1:
+            finish(chunk - 1)
+        if chunk == 2:
+            pass_on(0, 1)
+        if chunk == 3:
+            pass_on(1, 1)
+            pass_on(0, 2)
+        if chunk == 4:
+            pass_on(1, 2)
+            pass_on(0, 3)
+            for step in range(1, tops):
+                here = mask_buf.at[lax.rem(z - step + tops, tops)]
+                remote(here, here, m_snd.at[step - 1], m_rcv.at[step - 1], me, z).wait_recv()
+    pass_on(1, 3)
+    attend(0)
+    finish(chunks - 1)
+    attend(1)
+
+    half = QHEADS // 2 * HEAD
+    part = half // PAIRS
+    for pair in range(PAIRS):
+        first = pl.multiple_of(core * half + pair * part, HEAD)
+        out[0, :, pl.ds(first, part)] = o_buf[core, pair]
+    for pair in range(PAIRS):
+        first = pl.multiple_of((1 - core) * half + pair * part, HEAD)
+        remote(o_buf.at[core, pair], o_in.at[pair], o_snd.at[pair], o_rcv.at[pair], sibling, z).wait_recv()
+        out[0, :, pl.ds(first, part)] = o_in[pair]
+    for copy in sends:
+        copy.wait_send()
+    for pair in range(PAIRS):
+        for step in range(tops):
+
+            @pl.when((z >= step) & (z < tops - 1))
+            def _():
+                kv_copy(pair, z - step).wait_send()
+
+
+def fused_body(
+    hidden,
+    norm_gain,
+    w_query,
+    w_key,
+    w_value,
+    bias_query,
+    bias_key,
+    bias_value,
+    kv_blocks,
+    block_counts,
+):
+    tops = lax.axis_size("ctx")
+    rows = hidden.shape[1]
+    depth = w_query.shape[0]
+    chunks = PAIRS + QHEADS // 4
+    halves = []
+    for half in range(2):
+        for pair in range(PAIRS):
+            first = (PAIRS * half + pair) * HEAD
+            halves += [bias_key[first : first + HEAD], bias_value[first : first + HEAD]]
+        first = half * (QHEADS // 2 * HEAD)
+        halves.append(bias_query[first : first + QHEADS // 2 * HEAD])
+    bias = jnp.concatenate(halves).astype(jnp.float32).reshape(2 * chunks, 1, CHUNK)
+    position = (lax.axis_index("ctx") * rows + jnp.arange(rows, dtype=jnp.int32)).astype(jnp.float32)
+    exponent = (jnp.arange(HEAD) % (HEAD // 2)).astype(jnp.float32) * (2.0 / HEAD)
+    angles = position[:, None] * jnp.power(jnp.float32(THETA), -exponent)[None, :]
+    cosine = jnp.cos(angles)
+    sine = jnp.sin(angles) * jnp.where(jnp.arange(HEAD) < HEAD // 2, -1.0, 1.0)
+    slots = jnp.arange(MAXB)
+    active = (slots > 0) & (slots < block_counts[:, :, None])
+    seen = jnp.any(active[..., None] & (kv_blocks[..., None] == jnp.arange(tops)), axis=2)
+    seen = seen.transpose(1, 0, 2).reshape(tops, GROUP * tops, 1).astype(jnp.float32)
+    allowed = jnp.broadcast_to(seen, (tops, GROUP * tops, HEAD))
+    bf16, f32 = jnp.bfloat16, jnp.float32
+    vmem = pl.BlockSpec(memory_space=pltpu.VMEM)
+    hbm = pl.BlockSpec(memory_space=pl.ANY)
+    dma = pltpu.SemaphoreType.DMA
+    copies = 2 * PAIRS + chunks - PAIRS
+    part = QHEADS // 2 * HEAD // PAIRS
+    return pl.pallas_call(
+        fused_kernel,
+        out_shape=jax.ShapeDtypeStruct((1, rows, QHEADS * HEAD), bf16),
+        in_specs=[vmem, vmem, hbm, hbm, hbm, vmem, vmem, vmem, vmem],
+        out_specs=vmem,
+        scratch_shapes=[
+            pltpu.VMEM((3, rows, 2 * depth), bf16),
+            pltpu.VMEM((8, rows, 2 * depth), bf16),
+            pltpu.VMEM((chunks, 2 * depth, CHUNK), bf16),
+            pltpu.VMEM((chunks, 2, rows, CHUNK), bf16),
+            pltpu.VMEM((chunks, 2, rows, CHUNK), bf16),
+            pltpu.VMEM((chunks, 2, rows, CHUNK), bf16),
+            pltpu.VMEM((chunks, 2, rows, CHUNK), bf16),
+            pltpu.VMEM((chunks, rows, CHUNK), bf16),
+            pltpu.VMEM((chunks, rows, CHUNK), bf16),
+            pltpu.VMEM((chunks, rows, CHUNK), bf16),
+            pltpu.VMEM((chunks, rows, CHUNK), bf16),
+            pltpu.VMEM((chunks, 2, rows, CHUNK), f32),
+            pltpu.VMEM((chunks, 2, rows, CHUNK), f32),
+            pltpu.VMEM((tops, PAIRS, 2, rows, CHUNK), bf16),
+            pltpu.VMEM((2, QHEADS // 2, rows, HEAD), bf16),
+            pltpu.VMEM((tops, GROUP * tops, HEAD), f32),
+            pltpu.VMEM((GROUP * rows, HEAD), f32),
+            pltpu.VMEM((GROUP * rows, HEAD), f32),
+            pltpu.VMEM((2, PAIRS, rows, part), bf16),
+            pltpu.VMEM((PAIRS, rows, part), bf16),
+            dma((copies,)),
+            dma((copies,)),
+            dma((copies,)),
+            dma((3,)),
+            dma((3,)),
+            dma((4,)),
+            dma((4,)),
+            dma((tops - 1,)),
+            dma((tops - 1,)),
+            dma((2, chunks)),
+            dma((2, chunks)),
+            dma((2, chunks)),
+            dma((2, chunks)),
+            dma((PAIRS, tops)),
+            dma((PAIRS, tops)),
+            dma((PAIRS,)),
+            dma((PAIRS,)),
+        ],
+        compiler_params=pltpu.CompilerParams(
+            collective_id=0, has_side_effects=True, vmem_limit_bytes=40 * 1024 * 1024
+        ),
+    )(
+        hidden,
+        norm_gain.reshape(1, -1),
+        w_query,
+        w_key,
+        w_value,
+        bias,
+        cosine,
+        sine,
+        allowed,
+    )
+
+
 def solution(mesh):
     placed = (
         P("dp", "ctx", None),
@@ -158,6 +592,7 @@
         P("ctx", None, None),
         P("ctx", None),
     )
+    plane = mesh.shape["dp"] == 8 and mesh.shape["ctx"] == MAXB
     return jax.shard_map(
-        body, mesh=mesh, in_specs=placed, out_specs=P("dp", "ctx", None), check_vma=False
-    )
+        fused_body if plane else body, mesh=mesh, in_specs=placed, out_specs=P("dp", "ctx", None), check_vma=False
+    )

time: 172 us -> 67.7 us (0.39)
  the two profiles are of different devices: /device:TPU:0 before, /device:TPU:25 now
where the time goes in v2:
time: 67.7 us; the launch traced here: 67.2 us
  Pallas kernels  54 us (80%)
  local copies, waits for them, and re-layouts  11.2 us (17%)
  other arithmetic  1.91 us (3%)
    pallas_call x1, Pallas kernels, fused_body(): pl.pallas_call(fused_kernel, out_shape=jax.ShapeDtypeStruct((1, rows, QHE...  54 us
    unnamed x18, local copies, waits for them, and re-layouts  7.33 us
    slice x2, local copies, waits for them, and re-layouts, fused_body(): halves += [bias_key[first:first + HEAD], bias_value[first:first + HEAD]]  1.66 us

profile of v2, /device:TPU:25, one launch (start us, length us, event | category | flops | bytes accessed | tf_op | source)
XLA Modules:
  0.0 67.2 jit_solution(17878566486595461297)
XLA Ops:
  0.0 0.8 %fusion.3 = pred[4,4,4]{2,1,0:T(4,128)(4,1)S(1)} fusion(s32[4,4]{1,0:T(4,128)} %param.19, pred[4]{0:T(512)(128)(4,1)S(1)} %iota_compare_fusion.2), kind=kLoop, calls=%fused_computation.8 | loop fusion | flops 128 | bytes 132 | tf_op jit(solution)/shard_map/and | solution.py:512
  0.8 0.8 %fusion.2 = pred[4,4,4]{2,1,0:T(4,128)(4,1)S(1)} fusion(s32[4,4,4]{2,1,0:T(4,128)} %param.18, pred[4,4,4]{2,1,0:T(4,128)(4,1)S(1)} %fusion.3), kind=kLoop, calls=%fused_computation.5 | loop fusion | flops 704 | bytes 384 | tf_op jit(solution)/shard_map/reduce_or | solution.py:513
  1.6 0.7 %slice.34 = bf16[1024]{0:T(1024)(128)(2,1)S(1)} slice(bf16[2048]{0:T(1024)(128)(2,1)} %param.15), slice={[0:1024]} | slice | bytes 4096 | tf_op jit(solution)/shard_map/slice | solution.py:504
  2.3 0.8 %fusion.9 = (bf16[128]{0:T(256)(128)(2,1)S(1)}, bf16[128]{0:T(256)(128)(2,1)S(1)}, bf16[128]{0:T(256)(128)(2,1)S(1)}, bf16[128]{0:T(256)(128)(2,1)S(1)}) fusion(bf16[512]{0:T(512)(128)(2,1)} %param.16), kind=kLoop, calls=%fused_computation.19 | loop fusion | bytes 2048 | tf_op jit(solution)/shard_map/slice | solution.py:502
  3.1 0.8 %fusion.8 = (bf16[128]{0:T(256)(128)(2,1)S(1)}, bf16[128]{0:T(256)(128)(2,1)S(1)}, bf16[128]{0:T(256)(128)(2,1)S(1)}, bf16[128]{0:T(256)(128)(2,1)S(1)}) fusion(bf16[512]{0:T(512)(128)(2,1)} %param.17), kind=kLoop, calls=%fused_computation.18 | loop fusion | bytes 2048 | tf_op jit(solution)/shard_map/slice | solution.py:502
  4.0 0.1 reshape.61
  4.1 0.2 dynamic-update-slice
  4.2 0.2 dynamic-update-slice.1
  4.5 0.2 dynamic-update-slice.2
  4.7 0.2 dynamic-update-slice.3
  4.9 0.2 dynamic-update-slice.4
  5.1 0.2 dynamic-update-slice.5
  5.3 0.2 dynamic-update-slice.6
  5.5 0.2 dynamic-update-slice.7
  5.7 0.2 dynamic-update-slice.8
  5.9 0.7 %constant_dynamic-update-slice_fusion = bf16[3072]{0:T(1024)(128)(2,1)S(1)} fusion(bf16[3072]{0:T(1024)(128)(2,1)S(1)} %dynamic-update-slice.8, bf16[2048]{0:T(1024)(128)(2,1)} %param.15), kind=kLoop, calls=%fused_computation.9 | loop fusion | bytes 4096 | tf_op jit(solution)/shard_map/concatenate | solution.py:505
  6.6 0.7 %reshape.59.gain = bf16[1,3584]{1,0:T(2,128)(2,1)S(1)} reshape(bf16[3584]{0:T(1024)(128)(2,1)} %param.11) | data formatting | bytes 14336 | tf_op jit(solution)/shard_map/reshape | solution.py:571
  7.3 0.1 broadcast_in_dim.12.allowed
  7.4 0.3 fusion
  7.7 0.0 copy-start
  7.7 1.5 %copy-done = bf16[448,2048]{1,0:T(8,128)(2,1)S(1)} copy-done((bf16[448,2048]{1,0:T(8,128)(2,1)S(1)}, bf16[448,2048]{1,0:T(8,128)(2,1)}, u32[]{:S(2)}) %copy-start) | copy-done | bytes 1835032
  9.2 0.0 copy-start.1
  9.2 1.2 %copy-done.1 = bf16[1,128,3584]{2,1,0:T(8,128)(2,1)S(1)} copy-done((bf16[1,128,3584]{2,1,0:T(8,128)(2,1)S(1)}, bf16[1,128,3584]{2,1,0:T(8,128)(2,1)}, u32[]{:S(2)}) %copy-start.1) | copy-done | bytes 917528
  10.4 0.0 copy-start.2
  10.4 1.0 %copy-done.2 = bf16[448,512]{1,0:T(8,128)(2,1)S(1)} copy-done((bf16[448,512]{1,0:T(8,128)(2,1)S(1)}, bf16[448,512]{1,0:T(8,128)(2,1)}, u32[]{:S(2)}) %copy-start.2) | copy-done | bytes 458776
  11.4 0.0 copy-start.3
  11.4 1.0 %copy-done.3 = bf16[448,512]{1,0:T(8,128)(2,1)S(1)} copy-done((bf16[448,512]{1,0:T(8,128)(2,1)S(1)}, bf16[448,512]{1,0:T(8,128)(2,1)}, u32[]{:S(2)}) %copy-start.3) | copy-done | bytes 458776
  12.4 54.0 %shard_map.100 = bf16[1,128,2048]{2,1,0:T(8,128)(2,1)S(1)} custom-call(bf16[1,128,3584]{2,1,0:T(8,128)(2,1)S(1)} %copy-done.1, bf16[1,3584]{1,0:T(2,128)(2,1)S(1)} %reshape.59.gain, bf16[448,2048]{1,0:T(8,128)(2,1)S(1)} %copy-done, bf16[448,512]{1,0:T(8,128)(2,1)S(1)} %copy-done.2, bf16[448,512]{1,0:T(8,128)(2,1)S(1)} %copy-done.3, ...), custom_call_target="tpu_custom_call" | custom-call | tf_op jit(solution)/shard_map/pallas_call | solution.py:522
  66.4 0.8 %copy.23 = bf16[1,128,2048]{2,1,0:T(8,128)(2,1)} copy(bf16[1,128,2048]{2,1,0:T(8,128)(2,1)S(1)} %shard_map.100) | data formatting | bytes 1048576
  (7 shorter events, 0.0 us)
Async XLA Ops:
  7.7 1.5 %copy-start = (bf16[448,2048]{1,0:T(8,128)(2,1)S(1)}, bf16[448,2048]{1,0:T(8,128)(2,1)}, u32[]{:S(2)}) copy-start(bf16[448,2048]{1,0:T(8,128)(2,1)} %w_query.1) | copy-start | bytes 5505028
  9.2 1.2 %copy-start.1 = (bf16[1,128,3584]{2,1,0:T(8,128)(2,1)S(1)}, bf16[1,128,3584]{2,1,0:T(8,128)(2,1)}, u32[]{:S(2)}) copy-start(bf16[1,128,3584]{2,1,0:T(8,128)(2,1)} %hidden.1) | copy-start | bytes 2752516
  10.4 1.0 %copy-start.2 = (bf16[448,512]{1,0:T(8,128)(2,1)S(1)}, bf16[448,512]{1,0:T(8,128)(2,1)}, u32[]{:S(2)}) copy-start(bf16[448,512]{1,0:T(8,128)(2,1)} %w_key.1) | copy-start | bytes 1376260
  11.4 1.0 %copy-start.3 = (bf16[448,512]{1,0:T(8,128)(2,1)S(1)}, bf16[448,512]{1,0:T(8,128)(2,1)}, u32[]{:S(2)}) copy-start(bf16[448,512]{1,0:T(8,128)(2,1)} %w_value.1) | copy-start | bytes 1376260

commit v3 on v2

--- a/solution.py
+++ b/solution.py
@@ -1,3 +1,5 @@
+import math
+
 import jax
 import jax.numpy as jnp
 from jax import lax
@@ -167,11 +169,18 @@
     w_query,
     w_key,
     w_value,
-    bias,
+    bias_query,
+    bias_key,
+    bias_value,
+    kv_blocks,
+    block_counts,
+    out,
+    raw,
+    gains,
+    biases,
     cosine,
     sine,
     allowed,
-    out,
     normed,
     x_buf,
     w_buf,
@@ -192,6 +201,7 @@
     tot,
     o_buf,
     o_in,
+    h_sem,
     w_loc,
     w_snd,
     w_rcv,
@@ -226,6 +236,14 @@
     weights = (w_query, w_key, w_value)
     sends = []
 
+    read = pltpu.make_async_copy(hidden.at[0], raw, h_sem)
+    read.start()
+    barrier = pltpu.get_barrier_semaphore()
+    for peer in (sibling, xn, yn, dn):
+        pl.semaphore_signal(barrier, inc=1, device_id=(peer, z), device_id_type=MESH)
+    for step in range(1, tops):
+        pl.semaphore_signal(barrier, inc=1, device_id=(me, lax.rem(z + step, tops)), device_id_type=MESH)
+
     def remote(src, dst, snd, rcv, dp, ctx):
         return pltpu.make_async_remote_copy(
             src_ref=src, dst_ref=dst, send_sem=snd, recv_sem=rcv, device_id=(dp, ctx), device_id_type=MESH
@@ -250,24 +268,22 @@
             locals_.append((chunk, copy))
             number += 1
 
-    barrier = pltpu.get_barrier_semaphore()
-    for peer in (sibling, xn, yn, dn):
-        pl.semaphore_signal(barrier, inc=1, device_id=(peer, z), device_id_type=MESH)
-    for step in range(1, tops):
-        pl.semaphore_signal(barrier, inc=1, device_id=(me, lax.rem(z + step, tops)), device_id_type=MESH)
-
-    floats = hidden[0].astype(jnp.float32)
+    gains[...] = gain[...].astype(jnp.float32).reshape(1, -1)
+    read.wait()
+    floats = raw[...].astype(jnp.float32)
     scale = lax.rsqrt(jnp.mean(floats * floats, axis=-1, keepdims=True) + EPSILON)
-    pl.semaphore_wait(barrier, 4 + tops - 1)
 
     def norm_block(chip):
         cols = pl.ds(pl.multiple_of(chip * width, HEAD), width)
-        block = hidden[0, :, cols].astype(jnp.float32)
-        return (block * scale * gain[:, cols].astype(jnp.float32)).astype(jnp.bfloat16)
-
+        return (raw[:, cols].astype(jnp.float32) * scale * gains[:, cols]).astype(jnp.bfloat16)
+
+    normed[1] = norm_block(xn // 2)
+    pl.semaphore_wait(barrier, 4 + tops - 1)
     relations = (dn, xn, yn)
-    for index, peer in enumerate(relations):
-        normed[index] = norm_block(peer // 2)
+    for index in (1, 2, 0):
+        peer = relations[index]
+        if index != 1:
+            normed[index] = norm_block(peer // 2)
         launch(normed.at[index], x_buf.at[me], x_snd.at[index], x_rcv.at[index], peer, z)
     x_buf[me] = norm_block(me // 2)
     launch(x_buf.at[me], x_buf.at[me], f_snd.at[3], f_rcv.at[3], sibling, z)
@@ -284,10 +300,41 @@
                 z,
             )
             number += 1
+    for h in range(GROUP):
+        for b in range(tops):
+            blocks = kv_blocks[h, b : b + 1, :]
+            count = block_counts[h : h + 1, b : b + 1]
+            origin = lax.broadcasted_iota(jnp.int32, (tops, HEAD), 0)
+            seen = jnp.zeros((tops, HEAD), jnp.float32)
+            for slot in range(1, MAXB):
+                hit = (blocks[:, slot : slot + 1] == origin) & (count > slot)
+                seen = jnp.where(hit, 1.0, seen)
+            allowed[b, h * tops : (h + 1) * tops, :] = seen
     for step in range(1, tops):
         peer = lax.rem(z + step, tops)
         launch(allowed.at[peer], mask_buf.at[z], m_snd.at[step - 1], m_rcv.at[step - 1], me, peer)
     mask_buf[z] = allowed[z]
+
+    lane = lax.broadcasted_iota(jnp.int32, (BLOCK, HEAD), 1)
+    token = lax.broadcasted_iota(jnp.int32, (BLOCK, HEAD), 0) + z * BLOCK
+    exponent = lax.rem(lane, HEAD // 2).astype(jnp.float32) * (2.0 / HEAD)
+    angles = token.astype(jnp.float32) * jnp.exp(exponent * (-math.log(THETA)))
+    cosine[...] = jnp.cos(angles)
+    sine[...] = jnp.where(lane < HEAD // 2, -jnp.sin(angles), jnp.sin(angles))
+    starts = []
+    for vector in (bias_query, bias_key, bias_value):
+        first = starts[-1][1] if starts else 0
+        starts.append((first, first + vector.shape[0]))
+        biases[:, first : first + vector.shape[0]] = vector[...].astype(jnp.float32).reshape(1, -1)
+
+    def bias_of(chunk):
+        return jnp.concatenate(
+            [
+                biases[:, pl.ds(pl.multiple_of(starts[which][0] + first, HEAD), cols)]
+                for which, first, cols, _ in chunk_sources(core, chunk)
+            ],
+            axis=1,
+        )
 
     def sibling_of(device):
         return device + 1 - 2 * core
@@ -318,38 +365,53 @@
         pair = x_buf[pl.ds(device // 2 * 2, 2)].reshape(2 * BLOCK, width)
         return jnp.dot(pair, w_buf[chunk], preferred_element_type=jnp.float32)
 
-    def multiply(chunk):
-        wait_weights(chunk)
-        if chunk == 0:
-            forwarded(3, me)
-            docs_of(1)
-            docs_of(2)
-            docs_of(0)
-            forwarded(1, xn)
+    def first_x(chunk):
         to_x = product(chunk, xn)
         a1_out[chunk, 0] = to_x[:BLOCK].astype(jnp.bfloat16)
         keep[chunk, 1] = to_x[BLOCK:]
-        if chunk == 0:
-            forwarded(2, yn)
+        first_copy(0, 0, chunk).start()
+
+    def first_y(chunk):
         to_y = product(chunk, yn)
         b1_out[chunk, 0] = to_y[BLOCK:].astype(jnp.bfloat16)
         keep[chunk, 0] = to_y[:BLOCK]
-        if chunk == 0:
-            forwarded(0, dn)
+        first_copy(1, 0, chunk).start()
+
+    def first_d(chunk):
         to_d = product(chunk, dn).astype(jnp.bfloat16)
         a1_out[chunk, 1] = to_d[:BLOCK]
         b1_out[chunk, 1] = to_d[BLOCK:]
-        launch(a1_out.at[chunk], a1_in.at[chunk], s1_snd.at[0, chunk], s1_rcv.at[0, chunk], xn, z)
-        launch(b1_out.at[chunk], b1_in.at[chunk], s1_snd.at[1, chunk], s1_rcv.at[1, chunk], yn, z)
+        first_copy(0, 1, chunk).start()
+        first_copy(1, 1, chunk).start()
+
+    def first_own(chunk):
         mine = product(chunk, me)
         own[chunk, 0] = mine[:BLOCK]
         own[chunk, 1] = mine[BLOCK:]
 
+    def first_copy(doc, piece, chunk):
+        there, back = ((a1_out, a1_in), (b1_out, b1_in))[doc]
+        return remote(
+            there.at[chunk, piece],
+            back.at[chunk, piece],
+            s1_snd.at[doc, piece, chunk],
+            s1_rcv.at[doc, piece, chunk],
+            (xn, yn)[doc],
+            z,
+        )
+
+    def multiply(chunk):
+        wait_weights(chunk)
+        first_d(chunk)
+        first_x(chunk)
+        first_y(chunk)
+        first_own(chunk)
+
     def second(chunk):
-        remote(a1_out.at[chunk], a1_in.at[chunk], s1_snd.at[0, chunk], s1_rcv.at[0, chunk], xn, z).wait_recv()
+        first_copy(0, 1, chunk).wait_recv()
         a2_out[chunk] = (keep[chunk, 0] + a1_in[chunk, 1].astype(jnp.float32)).astype(jnp.bfloat16)
         launch(a2_out.at[chunk], a2_in.at[chunk], s2_snd.at[0, chunk], s2_rcv.at[0, chunk], yn, z)
-        remote(b1_out.at[chunk], b1_in.at[chunk], s1_snd.at[1, chunk], s1_rcv.at[1, chunk], yn, z).wait_recv()
+        first_copy(1, 1, chunk).wait_recv()
         b2_out[chunk] = (keep[chunk, 1] + b1_in[chunk, 1].astype(jnp.float32)).astype(jnp.bfloat16)
         launch(b2_out.at[chunk], b2_in.at[chunk], s2_snd.at[1, chunk], s2_rcv.at[1, chunk], xn, z)
 
@@ -362,7 +424,9 @@
 
     def finish(chunk):
         both = ((a1_in, a2_in, a2_out, yn), (b1_in, b2_in, b2_out, xn))
+        bias = bias_of(chunk)
         for doc, (first_in, second_in, second_out, peer) in enumerate(both):
+            first_copy(doc, 0, chunk).wait_recv()
             remote(
                 second_out.at[chunk], second_in.at[chunk], s2_snd.at[doc, chunk], s2_rcv.at[doc, chunk], peer, z
             ).wait_recv()
@@ -370,7 +434,7 @@
                 own[chunk, doc]
                 + first_in[chunk, 0].astype(jnp.float32)
                 + second_in[chunk].astype(jnp.float32)
-                + bias[core * chunks + chunk]
+                + bias
             )
             if chunk < PAIRS:
                 kv_buf[z, chunk, doc, :, :HEAD] = rotate(total[:, :HEAD])
@@ -399,76 +463,124 @@
             queries, keys, (((1,), (1,)), ((), ())), preferred_element_type=jnp.float32
         ) * HEAD ** (-0.5)
 
-    def attend(pair):
-        row = lax.broadcasted_iota(jnp.int32, (BLOCK, BLOCK), 0)
-        column = lax.broadcasted_iota(jnp.int32, (BLOCK, BLOCK), 1)
-        causal = jnp.concatenate([column <= row] * GROUP, axis=0)
+    row = lax.broadcasted_iota(jnp.int32, (BLOCK, BLOCK), 0)
+    column = lax.broadcasted_iota(jnp.int32, (BLOCK, BLOCK), 1)
+    causal = jnp.concatenate([column <= row] * 2, axis=0)
+
+    def attend_own(chunk):
+        at = chunk - PAIRS
         for doc in range(2):
-            queries = q_buf[doc, pair * GROUP : (pair + 1) * GROUP].reshape(GROUP * BLOCK, HEAD)
-            block = kv_buf[z, pair, doc]
+            queries = q_buf[doc, 2 * at : 2 * at + 2].reshape(2 * BLOCK, HEAD)
+            block = kv_buf[z, at // 2, doc]
             expo = jnp.where(causal, jnp.exp(scores_of(queries, block[:, :HEAD])), 0.0)
-            tot[...] = expo
-            acc[...] = jnp.dot(
+            tot[at, doc] = expo
+            acc[at, doc] = jnp.dot(
                 expo.astype(jnp.bfloat16), block[:, HEAD:], preferred_element_type=jnp.float32
             )
-            for origin in range(tops - 1):
-
-                @pl.when(origin < z)
-                def _():
-                    block = kv_buf[origin, pair, doc]
-                    flags = mask_buf[PAIRS * core + pair]
-                    seen = jnp.concatenate(
-                        [
-                            jnp.broadcast_to(flags[h * tops + origin : h * tops + origin + 1], (BLOCK, BLOCK))
-                            for h in range(GROUP)
-                        ],
-                        axis=0,
-                    )
-                    expo = jnp.where(seen > 0.5, jnp.exp(scores_of(queries, block[:, :HEAD])), 0.0)
-                    tot[...] += expo
-                    acc[...] += jnp.dot(
-                        expo.astype(jnp.bfloat16), block[:, HEAD:], preferred_element_type=jnp.float32
-                    )
-
-            mixed = (acc[...] / jnp.sum(tot[...], axis=-1, keepdims=True)).astype(jnp.bfloat16)
-            for h in range(GROUP):
-                first = h * HEAD
-                o_buf[doc, pair, :, first : first + HEAD] = mixed[h * BLOCK : (h + 1) * BLOCK]
-        launch(o_buf.at[1 - core, pair], o_in.at[pair], o_snd.at[pair], o_rcv.at[pair], sibling, z)
-
-    multiply(0)
-    multiply(1)
-    for chunk in range(chunks):
-        second(chunk)
-        if chunk + 2 < chunks:
-            multiply(chunk + 2)
-        if chunk >= 1:
-            finish(chunk - 1)
-        if chunk == 2:
-            pass_on(0, 1)
-        if chunk == 3:
-            pass_on(1, 1)
-            pass_on(0, 2)
-        if chunk == 4:
-            pass_on(1, 2)
-            pass_on(0, 3)
-            for step in range(1, tops):
-                here = mask_buf.at[lax.rem(z - step + tops, tops)]
-                remote(here, here, m_snd.at[step - 1], m_rcv.at[step - 1], me, z).wait_recv()
+
+    def attend_below(chunk, step):
+        at = chunk - PAIRS
+
+        @pl.when(z >= step)
+        def _():
+            origin = z - step
+            rows_of = [
+                mask_buf[PAIRS * core + at // 2, pl.ds((at % 2 * 2 + h) * tops + origin, 1)]
+                for h in range(2)
+            ]
+            seen = jnp.concatenate([jnp.broadcast_to(r, (BLOCK, BLOCK)) for r in rows_of], axis=0)
+            for doc in range(2):
+                queries = q_buf[doc, 2 * at : 2 * at + 2].reshape(2 * BLOCK, HEAD)
+                block = kv_buf[origin, at // 2, doc]
+                expo = jnp.where(seen > 0.5, jnp.exp(scores_of(queries, block[:, :HEAD])), 0.0)
+                tot[at, doc] += expo
+                acc[at, doc] += jnp.dot(
+                    expo.astype(jnp.bfloat16), block[:, HEAD:], preferred_element_type=jnp.float32
+                )
+
+    def attend_end(chunk):
+        at = chunk - PAIRS
+        for doc in range(2):
+            mixed = (acc[at, doc] / jnp.sum(tot[at, doc], axis=-1, keepdims=True)).astype(jnp.bfloat16)
+            o_buf[doc, at, :, :HEAD] = mixed[:BLOCK]
+            o_buf[doc, at, :, HEAD:] = mixed[BLOCK:]
+        launch(o_buf.at[1 - core, at], o_in.at[at], o_snd.at[at], o_rcv.at[at], sibling, z)
+
+    wait_weights(0)
+    wait_weights(1)
+    forwarded(3, me)
+    docs_of(1)
+    docs_of(2)
+    forwarded(1, xn)
+    first_x(0)
+    first_x(1)
+    forwarded(2, yn)
+    first_y(0)
+    first_y(1)
+    docs_of(0)
+    first_own(0)
+    forwarded(0, dn)
+    first_d(0)
+    first_d(1)
+    first_own(1)
+    second(0)
+    second(1)
+    multiply(2)
+    finish(0)
+    multiply(3)
+    finish(1)
+    second(2)
+    pass_on(0, 1)
+    multiply(4)
+    for step in range(1, tops):
+        here = mask_buf.at[lax.rem(z - step + tops, tops)]
+        remote(here, here, m_snd.at[step - 1], m_rcv.at[step - 1], me, z).wait_recv()
+    second(3)
+    multiply(5)
+    pass_on(1, 1)
+    finish(2)
+    attend_own(2)
+    attend_below(2, 1)
+    pass_on(0, 2)
+    attend_below(2, 2)
+    second(4)
+    finish(3)
+    attend_own(3)
+    attend_below(3, 1)
+    pass_on(1, 2)
+    attend_below(3, 2)
+    second(5)
+    pass_on(0, 3)
+    attend_below(2, 3)
+    attend_end(2)
+    attend_below(3, 3)
+    attend_end(3)
+    finish(4)
+    attend_own(4)
+    attend_below(4, 1)
+    attend_below(4, 2)
+    finish(5)
+    attend_own(5)
+    attend_below(5, 1)
+    attend_below(5, 2)
     pass_on(1, 3)
-    attend(0)
-    finish(chunks - 1)
-    attend(1)
+    attend_below(4, 3)
+    attend_end(4)
+    attend_below(5, 3)
+    attend_end(5)
 
     half = QHEADS // 2 * HEAD
-    part = half // PAIRS
-    for pair in range(PAIRS):
-        first = pl.multiple_of(core * half + pair * part, HEAD)
-        out[0, :, pl.ds(first, part)] = o_buf[core, pair]
-    for pair in range(PAIRS):
-        first = pl.multiple_of((1 - core) * half + pair * part, HEAD)
-        remote(o_buf.at[core, pair], o_in.at[pair], o_snd.at[pair], o_rcv.at[pair], sibling, z).wait_recv()
-        out[0, :, pl.ds(first, part)] = o_in[pair]
+    for at in range(chunks - PAIRS):
+        first = pl.multiple_of(core * half + at * CHUNK, CHUNK)
+        out[0, :, pl.ds(first, CHUNK)] = o_buf[core, at]
+    for at in range(chunks - PAIRS):
+        first = pl.multiple_of((1 - core) * half + at * CHUNK, CHUNK)
+        remote(o_buf.at[core, at], o_in.at[at], o_snd.at[at], o_rcv.at[at], sibling, z).wait_recv()
+        out[0, :, pl.ds(first, CHUNK)] = o_in[at]
+    for doc in range(2):
+        for piece in range(2):
+            for chunk in range(chunks):
+                first_copy(doc, piece, chunk).wait_send()
     for copy in sends:
         copy.wait_send()
     for pair in range(PAIRS):
@@ -495,36 +607,23 @@
     rows = hidden.shape[1]
     depth = w_query.shape[0]
     chunks = PAIRS + QHEADS // 4
-    halves = []
-    for half in range(2):
-        for pair in range(PAIRS):
-            first = (PAIRS * half + pair) * HEAD
-            halves += [bias_key[first : first + HEAD], bias_value[first : first + HEAD]]
-        first = half * (QHEADS // 2 * HEAD)
-        halves.append(bias_query[first : first + QHEADS // 2 * HEAD])
-    bias = jnp.concatenate(halves).astype(jnp.float32).reshape(2 * chunks, 1, CHUNK)
-    position = (lax.axis_index("ctx") * rows + jnp.arange(rows, dtype=jnp.int32)).astype(jnp.float32)
-    exponent = (jnp.arange(HEAD) % (HEAD // 2)).astype(jnp.float32) * (2.0 / HEAD)
-    angles = position[:, None] * jnp.power(jnp.float32(THETA), -exponent)[None, :]
-    cosine = jnp.cos(angles)
-    sine = jnp.sin(angles) * jnp.where(jnp.arange(HEAD) < HEAD // 2, -1.0, 1.0)
-    slots = jnp.arange(MAXB)
-    active = (slots > 0) & (slots < block_counts[:, :, None])
-    seen = jnp.any(active[..., None] & (kv_blocks[..., None] == jnp.arange(tops)), axis=2)
-    seen = seen.transpose(1, 0, 2).reshape(tops, GROUP * tops, 1).astype(jnp.float32)
-    allowed = jnp.broadcast_to(seen, (tops, GROUP * tops, HEAD))
     bf16, f32 = jnp.bfloat16, jnp.float32
     vmem = pl.BlockSpec(memory_space=pltpu.VMEM)
     hbm = pl.BlockSpec(memory_space=pl.ANY)
     dma = pltpu.SemaphoreType.DMA
     copies = 2 * PAIRS + chunks - PAIRS
-    part = QHEADS // 2 * HEAD // PAIRS
     return pl.pallas_call(
         fused_kernel,
         out_shape=jax.ShapeDtypeStruct((1, rows, QHEADS * HEAD), bf16),
-        in_specs=[vmem, vmem, hbm, hbm, hbm, vmem, vmem, vmem, vmem],
+        in_specs=[hbm, vmem, hbm, hbm, hbm, vmem, vmem, vmem, vmem, vmem],
         out_specs=vmem,
         scratch_shapes=[
+            pltpu.VMEM((rows, hidden.shape[2]), bf16),
+            pltpu.VMEM((1, hidden.shape[2]), f32),
+            pltpu.VMEM((1, (QHEADS + 2 * KVH) * HEAD), f32),
+            pltpu.VMEM((rows, HEAD), f32),
+            pltpu.VMEM((rows, HEAD), f32),
+            pltpu.VMEM((tops, GROUP * tops, HEAD), f32),
             pltpu.VMEM((3, rows, 2 * depth), bf16),
             pltpu.VMEM((8, rows, 2 * depth), bf16),
             pltpu.VMEM((chunks, 2 * depth, CHUNK), bf16),
@@ -541,10 +640,11 @@
             pltpu.VMEM((tops, PAIRS, 2, rows, CHUNK), bf16),
             pltpu.VMEM((2, QHEADS // 2, rows, HEAD), bf16),
             pltpu.VMEM((tops, GROUP * tops, HEAD), f32),
-            pltpu.VMEM((GROUP * rows, HEAD), f32),
-            pltpu.VMEM((GROUP * rows, HEAD), f32),
-            pltpu.VMEM((2, PAIRS, rows, part), bf16),
-            pltpu.VMEM((PAIRS, rows, part), bf16),
+            pltpu.VMEM((chunks - PAIRS, 2, 2 * rows, HEAD), f32),
+            pltpu.VMEM((chunks - PAIRS, 2, 2 * rows, HEAD), f32),
+            pltpu.VMEM((2, chunks - PAIRS, rows, CHUNK), bf16),
+            pltpu.VMEM((chunks - PAIRS, rows, CHUNK), bf16),
+            dma,
             dma((copies,)),
             dma((copies,)),
             dma((copies,)),
@@ -554,28 +654,29 @@
             dma((4,)),
             dma((tops - 1,)),
             dma((tops - 1,)),
-            dma((2, chunks)),
-            dma((2, chunks)),
+            dma((2, 2, chunks)),
+            dma((2, 2, chunks)),
             dma((2, chunks)),
             dma((2, chunks)),
             dma((PAIRS, tops)),
             dma((PAIRS, tops)),
-            dma((PAIRS,)),
-            dma((PAIRS,)),
+            dma((chunks - PAIRS,)),
+            dma((chunks - PAIRS,)),
         ],
         compiler_params=pltpu.CompilerParams(
-            collective_id=0, has_side_effects=True, vmem_limit_bytes=40 * 1024 * 1024
+            collective_id=0, has_side_effects=True, vmem_limit_bytes=60 * 1024 * 1024
         ),
     )(
         hidden,
-        norm_gain.reshape(1, -1),
+        norm_gain,
         w_query,
         w_key,
         w_value,
-        bias,
-        cosine,
-        sine,
-        allowed,
+        bias_query,
+        bias_key,
+        bias_value,
+        kv_blocks,
+        block_counts,
     )
 
 

time: 67.7 us -> 53.3 us (0.79)
  local copies, waits for them, and re-layouts: 11.2 us -> 1.88 us
  Pallas kernels: 54 us -> 50.6 us
  other arithmetic: 1.91 us -> 0 us
    unnamed x18 -> x1, local copies, waits for them, and re-layouts: 7.33 us -> 1.88 us
    pallas_call x1, Pallas kernels: 54 us -> 50.6 us  [fused_body(): pl.pallas_call(fused_kernel, out_shape=jax.ShapeDtypeStruct((1, rows, QHE...]
    slice x3 -> x0, local copies, waits for them, and re-layouts: 2.35 us -> none  [the longest x2 1.66 us: fused_body(): halves += [bias_key[first:first + HEAD], bias_value[first:first + HEAD]]]
    reduce_or x1 -> x0, other arithmetic: 0.81 us -> none  [fused_body(): jnp.any(active[..., None] & (kv_blocks[..., None] == jnp.arange(tops)), a...]
    and x1 -> x0, other arithmetic: 0.76 us -> none  [fused_body(): active = (slots > 0) & (slots < block_counts[:, :, None])]
    reshape x1 -> x0, local copies, waits for them, and re-layouts: 0.71 us -> none  [fused_body(): norm_gain.reshape(1, -1)]
    concatenate x1 -> x0, local copies, waits for them, and re-layouts: 0.69 us -> none  [fused_body(): jnp.concatenate(halves).astype(jnp.float32).reshape(2 * chunks, 1, CHUNK)]
where the time goes in v3:
time: 53.3 us; the launch traced here: 52.5 us
  Pallas kernels  50.6 us (95%)
  local copies, waits for them, and re-layouts  1.88 us (4%)
    pallas_call x1, Pallas kernels, fused_body(): pl.pallas_call(fused_kernel, out_shape=jax.ShapeDtypeStruct((1, rows, QHE...  50.6 us
    unnamed x1, local copies, waits for them, and re-layouts  1.88 us

profile of v3, /device:TPU:25, one launch (start us, length us, event | category | flops | bytes accessed | tf_op | source)
XLA Modules:
  0.0 52.5 jit_solution(14543800251618575601)
XLA Ops:
  0.0 50.6 %shard_map.100 = bf16[1,128,2048]{2,1,0:T(8,128)(2,1)} custom-call(bf16[1,128,3584]{2,1,0:T(8,128)(2,1)} %hidden.1, bf16[3584]{0:T(1024)(128)(2,1)} %gain.1, bf16[448,2048]{1,0:T(8,128)(2,1)} %w_query.1, bf16[448,512]{1,0:T(8,128)(2,1)} %w_key.1, bf16[448,512]{1,0:T(8,128)(2,1)} %w_value.1, bf16[2048]{0:T(1024)(128)(2,1)} %bias_query.1, ...), custom_call_target="tpu_custom_call" | custom-call | tf_op jit(solution)/shard_map/pallas_call | solution.py:615
  50.6 1.9 %copy.12 = bf16[1,128,2048]{2,1,0:T(8,128)(2,1)} copy(bf16[1,128,2048]{2,1,0:T(8,128)(2,1)} %shard_map.100) | data formatting | bytes 1048576

commit v4 on v3

--- a/solution.py
+++ b/solution.py
@@ -165,23 +165,31 @@
 
 def fused_kernel(
     hidden,
-    gain,
+    gain_hbm,
     w_query,
     w_key,
     w_value,
+    bias_query_hbm,
+    bias_key_hbm,
+    bias_value_hbm,
+    kv_blocks_hbm,
+    block_counts_hbm,
+    out,
+    gain,
     bias_query,
     bias_key,
     bias_value,
     kv_blocks,
     block_counts,
-    out,
     raw,
+    x_raw,
+    scale_out,
+    scale_in,
     gains,
     biases,
     cosine,
     sine,
     allowed,
-    normed,
     x_buf,
     w_buf,
     a1_out,
@@ -202,6 +210,9 @@
     o_buf,
     o_in,
     h_sem,
+    v_sem,
+    c_snd,
+    c_rcv,
     w_loc,
     w_snd,
     w_rcv,
@@ -238,6 +249,19 @@
 
     read = pltpu.make_async_copy(hidden.at[0], raw, h_sem)
     read.start()
+    smalls = []
+    for number, (source, place) in enumerate(
+        (
+            (gain_hbm, gain),
+            (kv_blocks_hbm, kv_blocks),
+            (block_counts_hbm, block_counts),
+            (bias_query_hbm, bias_query),
+            (bias_key_hbm, bias_key),
+            (bias_value_hbm, bias_value),
+        )
+    ):
+        smalls.append(pltpu.make_async_copy(source, place, v_sem.at[number]))
+        smalls[-1].start()
     barrier = pltpu.get_barrier_semaphore()
     for peer in (sibling, xn, yn, dn):
         pl.semaphore_signal(barrier, inc=1, device_id=(peer, z), device_id_type=MESH)
@@ -268,25 +292,15 @@
             locals_.append((chunk, copy))
             number += 1
 
-    gains[...] = gain[...].astype(jnp.float32).reshape(1, -1)
-    read.wait()
-    floats = raw[...].astype(jnp.float32)
-    scale = lax.rsqrt(jnp.mean(floats * floats, axis=-1, keepdims=True) + EPSILON)
-
-    def norm_block(chip):
-        cols = pl.ds(pl.multiple_of(chip * width, HEAD), width)
-        return (raw[:, cols].astype(jnp.float32) * scale * gains[:, cols]).astype(jnp.bfloat16)
-
-    normed[1] = norm_block(xn // 2)
+    def columns_of(chip):
+        return pl.ds(pl.multiple_of(chip * width, HEAD), width)
+
+    relations = (dn, xn, yn)
     pl.semaphore_wait(barrier, 4 + tops - 1)
-    relations = (dn, xn, yn)
     for index in (1, 2, 0):
         peer = relations[index]
-        if index != 1:
-            normed[index] = norm_block(peer // 2)
-        launch(normed.at[index], x_buf.at[me], x_snd.at[index], x_rcv.at[index], peer, z)
-    x_buf[me] = norm_block(me // 2)
-    launch(x_buf.at[me], x_buf.at[me], f_snd.at[3], f_rcv.at[3], sibling, z)
+        source = hidden.at[0, :, columns_of(peer // 2)]
+        launch(source, x_raw.at[index], x_snd.at[index], x_rcv.at[index], peer, z)
 
     number = 0
     for chunk in range(chunks):
@@ -300,6 +314,23 @@
                 z,
             )
             number += 1
+    row = lax.broadcasted_iota(jnp.int32, (BLOCK, BLOCK), 0)
+    column = lax.broadcasted_iota(jnp.int32, (BLOCK, BLOCK), 1)
+    read.wait()
+    floats = raw[...].astype(jnp.float32)
+    scale = lax.rsqrt(jnp.mean(floats * floats, axis=-1, keepdims=True) + EPSILON)
+    across = jnp.sum(jnp.where(row == column, scale, 0.0), axis=0, keepdims=True)
+    scale_out[...] = jnp.broadcast_to(across, scale_out.shape)
+    for index in (1, 2, 0):
+        launch(scale_out, scale_in.at[index], c_snd.at[index], c_rcv.at[index], relations[index], z)
+    smalls[0].wait()
+    gains[...] = gain[...].astype(jnp.float32).reshape(1, -1)
+    here = columns_of(me // 2)
+    x_buf[me] = (raw[:, here].astype(jnp.float32) * scale * gains[:, here]).astype(jnp.bfloat16)
+    launch(x_buf.at[me], x_buf.at[me], f_snd.at[3], f_rcv.at[3], sibling, z)
+
+    for copy in smalls[1:]:
+        copy.wait()
     for h in range(GROUP):
         for b in range(tops):
             blocks = kv_blocks[h, b : b + 1, :]
@@ -341,7 +372,13 @@
 
     def docs_of(index):
         peer = relations[index]
-        remote(x_buf.at[peer], x_buf.at[peer], x_snd.at[index], x_rcv.at[index], peer, z).wait_recv()
+        remote(scale_out, scale_in.at[index], c_snd.at[index], c_rcv.at[index], peer, z).wait_recv()
+        across = jnp.broadcast_to(scale_in[index, 0:1], (BLOCK, BLOCK))
+        scale = jnp.sum(jnp.where(row == column, across, 0.0), axis=1, keepdims=True)
+        remote(x_raw.at[index], x_raw.at[index], x_snd.at[index], x_rcv.at[index], peer, z).wait_recv()
+        x_buf[peer] = (
+            x_raw[index].astype(jnp.float32) * scale * gains[:, columns_of(me // 2)]
+        ).astype(jnp.bfloat16)
         launch(x_buf.at[peer], x_buf.at[peer], f_snd.at[index], f_rcv.at[index], sibling, z)
 
     def forwarded(index, device):
@@ -463,8 +500,6 @@
             queries, keys, (((1,), (1,)), ((), ())), preferred_element_type=jnp.float32
         ) * HEAD ** (-0.5)
 
-    row = lax.broadcasted_iota(jnp.int32, (BLOCK, BLOCK), 0)
-    column = lax.broadcasted_iota(jnp.int32, (BLOCK, BLOCK), 1)
     causal = jnp.concatenate([column <= row] * 2, axis=0)
 
     def attend_own(chunk):
@@ -506,17 +541,17 @@
             o_buf[doc, at, :, HEAD:] = mixed[BLOCK:]
         launch(o_buf.at[1 - core, at], o_in.at[at], o_snd.at[at], o_rcv.at[at], sibling, z)
 
-    wait_weights(0)
-    wait_weights(1)
+    for chunk in range(3):
+        wait_weights(chunk)
     forwarded(3, me)
     docs_of(1)
     docs_of(2)
     forwarded(1, xn)
-    first_x(0)
-    first_x(1)
+    for chunk in range(3):
+        first_x(chunk)
     forwarded(2, yn)
-    first_y(0)
-    first_y(1)
+    for chunk in range(3):
+        first_y(chunk)
     docs_of(0)
     first_own(0)
     forwarded(0, dn)
@@ -525,8 +560,9 @@
     first_own(1)
     second(0)
     second(1)
-    multiply(2)
+    first_d(2)
     finish(0)
+    first_own(2)
     multiply(3)
     finish(1)
     second(2)
@@ -614,17 +650,25 @@
     copies = 2 * PAIRS + chunks - PAIRS
     return pl.pallas_call(
         fused_kernel,
-        out_shape=jax.ShapeDtypeStruct((1, rows, QHEADS * HEAD), bf16),
-        in_specs=[hbm, vmem, hbm, hbm, hbm, vmem, vmem, vmem, vmem, vmem],
+        out_shape=pltpu.VMEM((1, rows, QHEADS * HEAD), bf16),
+        in_specs=[hbm] * 10,
         out_specs=vmem,
         scratch_shapes=[
+            pltpu.VMEM(norm_gain.shape, bf16),
+            pltpu.VMEM(bias_query.shape, bf16),
+            pltpu.VMEM(bias_key.shape, bf16),
+            pltpu.VMEM(bias_value.shape, bf16),
+            pltpu.VMEM(kv_blocks.shape, jnp.int32),
+            pltpu.VMEM(block_counts.shape, jnp.int32),
             pltpu.VMEM((rows, hidden.shape[2]), bf16),
+            pltpu.VMEM((3, rows, 2 * depth), bf16),
+            pltpu.VMEM((8, rows), f32),
+            pltpu.VMEM((3, 8, rows), f32),
             pltpu.VMEM((1, hidden.shape[2]), f32),
             pltpu.VMEM((1, (QHEADS + 2 * KVH) * HEAD), f32),
             pltpu.VMEM((rows, HEAD), f32),
             pltpu.VMEM((rows, HEAD), f32),
             pltpu.VMEM((tops, GROUP * tops, HEAD), f32),
-            pltpu.VMEM((3, rows, 2 * depth), bf16),
             pltpu.VMEM((8, rows, 2 * depth), bf16),
             pltpu.VMEM((chunks, 2 * depth, CHUNK), bf16),
             pltpu.VMEM((chunks, 2, rows, CHUNK), bf16),
@@ -645,6 +689,9 @@
             pltpu.VMEM((2, chunks - PAIRS, rows, CHUNK), bf16),
             pltpu.VMEM((chunks - PAIRS, rows, CHUNK), bf16),
             dma,
+            dma((6,)),
+            dma((3,)),
+            dma((3,)),
             dma((copies,)),
             dma((copies,)),
             dma((copies,)),
@@ -664,7 +711,7 @@
             dma((chunks - PAIRS,)),
         ],
         compiler_params=pltpu.CompilerParams(
-            collective_id=0, has_side_effects=True, vmem_limit_bytes=60 * 1024 * 1024
+            collective_id=0, has_side_effects=True, vmem_limit_bytes=56 * 1024 * 1024
         ),
     )(
         hidden,

time: 53.3 us -> 53.3 us (level); the launches traced: 52.5 us -> 53.1 us
  Pallas kernels: 50.6 us -> 52.3 us
  local copies, waits for them, and re-layouts: 1.88 us -> 0.8 us
    pallas_call x1, Pallas kernels: 50.6 us -> 52.3 us  [fused_body(): pl.pallas_call(fused_kernel, out_shape=pltpu.VMEM((1, rows, QHEADS * HEAD...]
    unnamed x1, local copies, waits for them, and re-layouts: 1.88 us -> 0.8 us
where the time goes in v4:
time: 53.3 us; the launch traced here: 53.1 us
  Pallas kernels  52.3 us (98%)
  local copies, waits for them, and re-layouts  0.8 us (2%)
    pallas_call x1, Pallas kernels, fused_body(): pl.pallas_call(fused_kernel, out_shape=pltpu.VMEM((1, rows, QHEADS * HEAD...  52.3 us

profile of v4, /device:TPU:25, one launch (start us, length us, event | category | flops | bytes accessed | tf_op | source)
XLA Modules:
  0.0 53.1 jit_solution(12169618216747704194)
XLA Ops:
  0.0 52.3 %shard_map.100 = bf16[1,128,2048]{2,1,0:T(8,128)(2,1)S(1)} custom-call(bf16[1,128,3584]{2,1,0:T(8,128)(2,1)} %hidden.1, bf16[3584]{0:T(1024)(128)(2,1)} %gain_hbm.1, bf16[448,2048]{1,0:T(8,128)(2,1)} %w_query.1, bf16[448,512]{1,0:T(8,128)(2,1)} %w_key.1, bf16[448,512]{1,0:T(8,128)(2,1)} %w_value.1, bf16[2048]{0:T(1024)(128)(2,1)} %bias_query_hbm.1, ...), custom_call_target="tpu_custom_call" | custom-call | tf_op jit(solution)/shard_map/pallas_call | solution.py:651
  52.4 0.8 %copy.12 = bf16[1,128,2048]{2,1,0:T(8,128)(2,1)} copy(bf16[1,128,2048]{2,1,0:T(8,128)(2,1)S(1)} %shard_map.100) | data formatting | bytes 1048576

commit v5 on v4

--- a/solution.py
+++ b/solution.py
@@ -297,23 +297,30 @@
 
     relations = (dn, xn, yn)
     pl.semaphore_wait(barrier, 4 + tops - 1)
-    for index in (1, 2, 0):
+
+    def send_raw(index):
         peer = relations[index]
         source = hidden.at[0, :, columns_of(peer // 2)]
         launch(source, x_raw.at[index], x_snd.at[index], x_rcv.at[index], peer, z)
 
-    number = 0
-    for chunk in range(chunks):
-        for which, first, cols, place in chunk_sources(1 - core, chunk):
-            launch(
-                weights[which].at[:, pl.ds(first, cols)],
-                w_buf.at[chunk, rows, pl.ds(place, cols)],
-                w_snd.at[number],
-                w_rcv.at[number],
-                sibling,
-                z,
-            )
-            number += 1
+    send_raw(1)
+    send_raw(2)
+
+    def send_weights(wanted):
+        number = 0
+        for chunk in range(chunks):
+            for which, first, cols, place in chunk_sources(1 - core, chunk):
+                if chunk in wanted:
+                    launch(
+                        weights[which].at[:, pl.ds(first, cols)],
+                        w_buf.at[chunk, rows, pl.ds(place, cols)],
+                        w_snd.at[number],
+                        w_rcv.at[number],
+                        sibling,
+                        z,
+                    )
+                number += 1
+
     row = lax.broadcasted_iota(jnp.int32, (BLOCK, BLOCK), 0)
     column = lax.broadcasted_iota(jnp.int32, (BLOCK, BLOCK), 1)
     read.wait()
@@ -323,12 +330,14 @@
     scale_out[...] = jnp.broadcast_to(across, scale_out.shape)
     for index in (1, 2, 0):
         launch(scale_out, scale_in.at[index], c_snd.at[index], c_rcv.at[index], relations[index], z)
+    send_raw(0)
     smalls[0].wait()
     gains[...] = gain[...].astype(jnp.float32).reshape(1, -1)
     here = columns_of(me // 2)
     x_buf[me] = (raw[:, here].astype(jnp.float32) * scale * gains[:, here]).astype(jnp.bfloat16)
     launch(x_buf.at[me], x_buf.at[me], f_snd.at[3], f_rcv.at[3], sibling, z)
 
+    send_weights((0, 1, 2))
     for copy in smalls[1:]:
         copy.wait()
     for h in range(GROUP):
@@ -406,25 +415,25 @@
         to_x = product(chunk, xn)
         a1_out[chunk, 0] = to_x[:BLOCK].astype(jnp.bfloat16)
         keep[chunk, 1] = to_x[BLOCK:]
-        first_copy(0, 0, chunk).start()
 
     def first_y(chunk):
         to_y = product(chunk, yn)
         b1_out[chunk, 0] = to_y[BLOCK:].astype(jnp.bfloat16)
         keep[chunk, 0] = to_y[:BLOCK]
-        first_copy(1, 0, chunk).start()
 
     def first_d(chunk):
         to_d = product(chunk, dn).astype(jnp.bfloat16)
         a1_out[chunk, 1] = to_d[:BLOCK]
         b1_out[chunk, 1] = to_d[BLOCK:]
-        first_copy(0, 1, chunk).start()
-        first_copy(1, 1, chunk).start()
 
     def first_own(chunk):
         mine = product(chunk, me)
         own[chunk, 0] = mine[:BLOCK]
         own[chunk, 1] = mine[BLOCK:]
+
+    def send_first(chunk, piece):
+        first_copy(0, piece, chunk).start()
+        first_copy(1, piece, chunk).start()
 
     def first_copy(doc, piece, chunk):
         there, back = ((a1_out, a1_in), (b1_out, b1_in))[doc]
@@ -438,7 +447,6 @@
         )
 
     def multiply(chunk):
-        wait_weights(chunk)
         first_d(chunk)
         first_x(chunk)
         first_y(chunk)
@@ -549,30 +557,43 @@
     forwarded(1, xn)
     for chunk in range(3):
         first_x(chunk)
+        first_copy(0, 0, chunk).start()
     forwarded(2, yn)
     for chunk in range(3):
         first_y(chunk)
+        first_copy(1, 0, chunk).start()
+    first_own(0)
     docs_of(0)
-    first_own(0)
+    send_weights(range(3, chunks))
+    first_own(1)
     forwarded(0, dn)
-    first_d(0)
-    first_d(1)
-    first_own(1)
+    for chunk in range(2):
+        first_d(chunk)
+        send_first(chunk, 1)
+    first_d(2)
+    first_own(2)
     second(0)
+    for chunk in range(3, chunks):
+        wait_weights(chunk)
     second(1)
-    first_d(2)
+    send_first(2, 1)
     finish(0)
-    first_own(2)
     multiply(3)
+    send_first(3, 1)
+    send_first(3, 0)
     finish(1)
+    multiply(4)
     second(2)
+    send_first(4, 1)
+    send_first(4, 0)
     pass_on(0, 1)
-    multiply(4)
+    multiply(5)
     for step in range(1, tops):
         here = mask_buf.at[lax.rem(z - step + tops, tops)]
         remote(here, here, m_snd.at[step - 1], m_rcv.at[step - 1], me, z).wait_recv()
     second(3)
-    multiply(5)
+    send_first(5, 1)
+    send_first(5, 0)
     pass_on(1, 1)
     finish(2)
     attend_own(2)
@@ -595,13 +616,13 @@
     attend_own(4)
     attend_below(4, 1)
     attend_below(4, 2)
+    pass_on(1, 3)
+    attend_below(4, 3)
+    attend_end(4)
     finish(5)
     attend_own(5)
     attend_below(5, 1)
     attend_below(5, 2)
-    pass_on(1, 3)
-    attend_below(4, 3)
-    attend_end(4)
     attend_below(5, 3)
     attend_end(5)
 

time: 53.3 us -> 49.9 us (0.936)
  Pallas kernels: 52.3 us -> 49 us
    pallas_call x1, Pallas kernels: 52.3 us -> 49 us  [fused_body(): pl.pallas_call(fused_kernel, out_shape=pltpu.VMEM((1, rows, QHEADS * HEAD...]
where the time goes in v5:
time: 49.9 us; the launch traced here: 49.8 us
  Pallas kernels  49 us (98%)
  local copies, waits for them, and re-layouts  0.8 us (2%)
    pallas_call x1, Pallas kernels, fused_body(): pl.pallas_call(fused_kernel, out_shape=pltpu.VMEM((1, rows, QHEADS * HEAD...  49 us

profile of v5, /device:TPU:25, one launch (start us, length us, event | category | flops | bytes accessed | tf_op | source)
XLA Modules:
  0.0 49.8 jit_solution(13660103795360814991)
XLA Ops:
  0.0 49.0 %shard_map.100 = bf16[1,128,2048]{2,1,0:T(8,128)(2,1)S(1)} custom-call(bf16[1,128,3584]{2,1,0:T(8,128)(2,1)} %hidden.1, bf16[3584]{0:T(1024)(128)(2,1)} %gain_hbm.1, bf16[448,2048]{1,0:T(8,128)(2,1)} %w_query.1, bf16[448,512]{1,0:T(8,128)(2,1)} %w_key.1, bf16[448,512]{1,0:T(8,128)(2,1)} %w_value.1, bf16[2048]{0:T(1024)(128)(2,1)} %bias_query_hbm.1, ...), custom_call_target="tpu_custom_call" | custom-call | tf_op jit(solution)/shard_map/pallas_call | solution.py:672
  49.0 0.8 %copy.12 = bf16[1,128,2048]{2,1,0:T(8,128)(2,1)} copy(bf16[1,128,2048]{2,1,0:T(8,128)(2,1)S(1)} %shard_map.100) | data formatting | bytes 1048576

commit v6 on v5

--- a/solution.py
+++ b/solution.py
@@ -591,25 +591,25 @@
     for step in range(1, tops):
         here = mask_buf.at[lax.rem(z - step + tops, tops)]
         remote(here, here, m_snd.at[step - 1], m_rcv.at[step - 1], me, z).wait_recv()
+    pass_on(1, 1)
     second(3)
     send_first(5, 1)
     send_first(5, 0)
-    pass_on(1, 1)
+    pass_on(0, 2)
     finish(2)
     attend_own(2)
     attend_below(2, 1)
-    pass_on(0, 2)
     attend_below(2, 2)
+    pass_on(1, 2)
     second(4)
     finish(3)
     attend_own(3)
     attend_below(3, 1)
-    pass_on(1, 2)
     attend_below(3, 2)
-    second(5)
     pass_on(0, 3)
     attend_below(2, 3)
     attend_end(2)
+    second(5)
     attend_below(3, 3)
     attend_end(3)
     finish(4)

time: 49.9 us -> 50.3 us (level)
  no operation moved by 1% of the time
where the time goes in v6:
time: 50.3 us; the launch traced here: 50.1 us
  Pallas kernels  49.3 us (98%)
  local copies, waits for them, and re-layouts  0.8 us (2%)
    pallas_call x1, Pallas kernels, fused_body(): pl.pallas_call(fused_kernel, out_shape=pltpu.VMEM((1, rows, QHEADS * HEAD...  49.3 us

profile of v6, /device:TPU:25, one launch (start us, length us, event | category | flops | bytes accessed | tf_op | source)
XLA Modules:
  0.0 50.1 jit_solution(1994396354614620482)
XLA Ops:
  0.0 49.3 %shard_map.100 = bf16[1,128,2048]{2,1,0:T(8,128)(2,1)S(1)} custom-call(bf16[1,128,3584]{2,1,0:T(8,128)(2,1)} %hidden.1, bf16[3584]{0:T(1024)(128)(2,1)} %gain_hbm.1, bf16[448,2048]{1,0:T(8,128)(2,1)} %w_query.1, bf16[448,512]{1,0:T(8,128)(2,1)} %w_key.1, bf16[448,512]{1,0:T(8,128)(2,1)} %w_value.1, bf16[2048]{0:T(1024)(128)(2,1)} %bias_query_hbm.1, ...), custom_call_target="tpu_custom_call" | custom-call | tf_op jit(solution)/shard_map/pallas_call | solution.py:672
  49.3 0.8 %copy.12 = bf16[1,128,2048]{2,1,0:T(8,128)(2,1)} copy(bf16[1,128,2048]{2,1,0:T(8,128)(2,1)S(1)} %shard_map.100) | data formatting | bytes 1048576

commit v7 on v5

--- a/solution.py
+++ b/solution.py
@@ -555,28 +555,31 @@
     docs_of(1)
     docs_of(2)
     forwarded(1, xn)
-    for chunk in range(3):
+    for chunk in range(2):
         first_x(chunk)
         first_copy(0, 0, chunk).start()
     forwarded(2, yn)
-    for chunk in range(3):
+    for chunk in range(2):
         first_y(chunk)
         first_copy(1, 0, chunk).start()
-    first_own(0)
+    first_x(2)
+    first_y(2)
     docs_of(0)
     send_weights(range(3, chunks))
-    first_own(1)
+    first_own(0)
     forwarded(0, dn)
     for chunk in range(2):
         first_d(chunk)
         send_first(chunk, 1)
+    first_own(1)
+    second(0)
+    send_first(2, 0)
     first_d(2)
-    first_own(2)
-    second(0)
     for chunk in range(3, chunks):
         wait_weights(chunk)
     second(1)
     send_first(2, 1)
+    first_own(2)
     finish(0)
     multiply(3)
     send_first(3, 1)

time: 49.9 us -> 49 us (0.982); the launches traced: 49.8 us -> 48.1 us
  Pallas kernels: 49 us -> 47.3 us
    pallas_call x1, Pallas kernels: 49 us -> 47.3 us  [fused_body(): pl.pallas_call(fused_kernel, out_shape=pltpu.VMEM((1, rows, QHEADS * HEAD...]
where the time goes in v7:
time: 49 us; the launch traced here: 48.1 us
  Pallas kernels  47.3 us (97%)
  local copies, waits for them, and re-layouts  0.8 us (2%)
    pallas_call x1, Pallas kernels, fused_body(): pl.pallas_call(fused_kernel, out_shape=pltpu.VMEM((1, rows, QHEADS * HEAD...  47.3 us

profile of v7, /device:TPU:25, one launch (start us, length us, event | category | flops | bytes accessed | tf_op | source)
XLA Modules:
  0.0 48.1 jit_solution(18125328797746982078)
XLA Ops:
  0.0 47.3 %shard_map.100 = bf16[1,128,2048]{2,1,0:T(8,128)(2,1)S(1)} custom-call(bf16[1,128,3584]{2,1,0:T(8,128)(2,1)} %hidden.1, bf16[3584]{0:T(1024)(128)(2,1)} %gain_hbm.1, bf16[448,2048]{1,0:T(8,128)(2,1)} %w_query.1, bf16[448,512]{1,0:T(8,128)(2,1)} %w_key.1, bf16[448,512]{1,0:T(8,128)(2,1)} %w_value.1, bf16[2048]{0:T(1024)(128)(2,1)} %bias_query_hbm.1, ...), custom_call_target="tpu_custom_call" | custom-call | tf_op jit(solution)/shard_map/pallas_call | solution.py:675
  47.3 0.8 %copy.12 = bf16[1,128,2048]{2,1,0:T(8,128)(2,1)} copy(bf16[1,128,2048]{2,1,0:T(8,128)(2,1)S(1)} %shard_map.100) | data formatting | bytes 1048576

commit v8 on v7

--- a/solution.py
+++ b/solution.py
@@ -579,12 +579,15 @@
         wait_weights(chunk)
     second(1)
     send_first(2, 1)
-    first_own(2)
     finish(0)
-    multiply(3)
+    first_d(3)
+    first_x(3)
+    first_y(3)
     send_first(3, 1)
     send_first(3, 0)
     finish(1)
+    first_own(2)
+    first_own(3)
     multiply(4)
     second(2)
     send_first(4, 1)

time: 49 us -> 49 us (level)
  no operation moved by 1% of the time
where the time goes in v8:
time: 49 us; the launch traced here: 48.1 us
  Pallas kernels  47.3 us (97%)
  local copies, waits for them, and re-layouts  0.8 us (2%)
    pallas_call x1, Pallas kernels, fused_body(): pl.pallas_call(fused_kernel, out_shape=pltpu.VMEM((1, rows, QHEADS * HEAD...  47.3 us

profile of v8, /device:TPU:25, one launch (start us, length us, event | category | flops | bytes accessed | tf_op | source)
XLA Modules:
  0.0 48.1 jit_solution(2789103315502868222)
XLA Ops:
  0.0 47.3 %shard_map.100 = bf16[1,128,2048]{2,1,0:T(8,128)(2,1)S(1)} custom-call(bf16[1,128,3584]{2,1,0:T(8,128)(2,1)} %hidden.1, bf16[3584]{0:T(1024)(128)(2,1)} %gain_hbm.1, bf16[448,2048]{1,0:T(8,128)(2,1)} %w_query.1, bf16[448,512]{1,0:T(8,128)(2,1)} %w_key.1, bf16[448,512]{1,0:T(8,128)(2,1)} %w_value.1, bf16[2048]{0:T(1024)(128)(2,1)} %bias_query_hbm.1, ...), custom_call_target="tpu_custom_call" | custom-call | tf_op jit(solution)/shard_map/pallas_call | solution.py:678
  47.3 0.8 %copy.12 = bf16[1,128,2048]{2,1,0:T(8,128)(2,1)} copy(bf16[1,128,2048]{2,1,0:T(8,128)(2,1)S(1)} %shard_map.100) | data formatting | bytes 1048576
